TPU v7x, 512 devices: a whole 4x8x8 slice. The times are simulated.
512 devices in a mesh: dom: 16 (over z, core), pencil: 32 (over x, y).
Axes of the slice: x: 4, y: 8, z: 8, core: 2. Of those that a mesh axis runs over, the one named last changes fastest.
Arguments:
- modes_now: float32 [16, 128, 512, 128], P('dom', 'pencil'), may hold values from -6 to 6
- modes_prev: float32 [16, 128, 512, 128], P('dom', 'pencil'), may hold values from -6 to 6
- extents: int32 [16], P('dom'), may hold values from 64 to 128, as said below
Outputs:
- pressure: float32 [16, 512, 128, 128], P('dom', 'pencil')
- modes_next: float32 [16, 128, 512, 128], P('dom', 'pencil')
Inputs may be any that keep to these rules, and one draw needn't show every extreme that they name: `extents`: some partition has exactly 128 live cells along x.
All inputs are finite; a program needn't handle non-finite values.
Results may differ from a plain program's by a relative error of at most 0.0003.
Values sent between devices are 32-bit elements; how exact they have to be, the bound alone decides.
A program may use at most 64 MiB of HBM per device.

v0:
```python
import jax
import jax.numpy as jnp
from jax import lax
from jax.sharding import PartitionSpec as P

HIGH = lax.Precision.HIGHEST
COEF_ONE = 1.5
COEF_TWO = -0.15
COEF_THREE = 1.0 / 90.0
STEP_DT = 0.5


def from_behind(block, axis, distance):
    devices = range(lax.axis_size(axis))
    route = [(i - distance, i) for i in devices if i - distance in devices]
    return lax.ppermute(block, axis, route)


def cosine_table(live, size):
    live = jnp.asarray(live, jnp.int32)
    mode_index = lax.broadcasted_iota(jnp.int32, (size, size), 0)
    cell_index = lax.broadcasted_iota(jnp.int32, (size, size), 1)
    phase_index = mode_index * (2 * cell_index + 1) % (4 * live)
    count = live.astype(jnp.float32)
    radians = jnp.pi * phase_index.astype(jnp.float32) / (2.0 * count)
    norm_factor = jnp.where(mode_index == 0, jnp.sqrt(1.0 / count), jnp.sqrt(2.0 / count))
    inside = (mode_index < live) & (cell_index < live)
    return jnp.where(inside, norm_factor * jnp.cos(radians), jnp.float32(0.0))


def face_forcing(own, other):
    diff = other - own
    first_layer = (
        COEF_ONE * diff[..., 0, :, :]
        + COEF_TWO * diff[..., 1, :, :]
        + COEF_THREE * diff[..., 2, :, :]
    )
    second_layer = COEF_TWO * diff[..., 0, :, :] + COEF_THREE * diff[..., 1, :, :]
    third_layer = COEF_THREE * diff[..., 0, :, :]
    return jnp.stack([first_layer, second_layer, third_layer], axis=-3)


def advance_modes(modes, earlier, forcing, extent, ky_start, size_y, size_z):
    shape = modes.shape
    mode_y = (ky_start + lax.broadcasted_iota(jnp.int32, shape, 0)).astype(jnp.float32)
    mode_z = lax.broadcasted_iota(jnp.int32, shape, 1).astype(jnp.float32)
    mode_x_int = lax.broadcasted_iota(jnp.int32, shape, 2)
    mode_x = mode_x_int.astype(jnp.float32)
    frequency = jnp.pi * jnp.sqrt(
        (mode_x / extent.astype(jnp.float32)) ** 2 + (mode_y / size_y) ** 2 + (mode_z / size_z) ** 2
    )
    gain_force = STEP_DT * STEP_DT * jnp.sinc(frequency * STEP_DT / (2.0 * jnp.pi)) ** 2
    advanced = 2.0 * jnp.cos(frequency * STEP_DT) * modes - earlier + gain_force * forcing
    return jnp.where(mode_x_int < extent, advanced, jnp.float32(0.0))


def local(modes_now, modes_prev, extents):
    modes = modes_now[0]
    earlier = modes_prev[0]
    extent = extents[0]
    rows_y = modes.shape[0]
    size_z = modes.shape[1]
    size_x = modes.shape[2]
    size_y = rows_y * lax.axis_size("pencil")
    table_z = cosine_table(size_z, size_z)
    table_y = cosine_table(size_y, size_y)
    table_x = cosine_table(extent, size_x)
    domain = lax.axis_index("dom")
    domains = lax.axis_size("dom")
    along_z = jnp.einsum("bck,cz->bzk", modes, table_z, precision=HIGH)
    along_y = jnp.einsum(
        "yzk,ya->zak",
        lax.all_to_all(along_z, "pencil", split_axis=1, concat_axis=0, tiled=True),
        table_y,
        precision=HIGH,
    )
    field = jnp.einsum("zyk,kx->zyx", along_y, table_x, precision=HIGH)
    lower_rim = jnp.moveaxis(field[:, :, 0:3], 2, 0)
    upper_block = lax.dynamic_slice_in_dim(field, extent - 3, 3, axis=2)
    upper_rim = jnp.moveaxis(upper_block, 2, 0)[::-1]
    from_lower = from_behind(upper_rim, "dom", 1)
    from_upper = from_behind(lower_rim, "dom", -1)
    lower_force = face_forcing(lower_rim, from_lower) * (domain > 0).astype(jnp.float32)
    upper_force = face_forcing(upper_rim, from_upper) * (domain < domains - 1).astype(jnp.float32)
    layers = jnp.concatenate([lower_force, upper_force], axis=0)
    offsets = jnp.arange(3, dtype=jnp.int32)
    positions = jnp.concatenate([offsets, extent - 1 - offsets])
    columns = lax.broadcasted_iota(jnp.int32, (6, size_x), 1)
    onehot = (columns == positions[:, None]).astype(jnp.float32)
    forcing_field = jnp.einsum("lzy,lx->zyx", layers, onehot, precision=HIGH)
    along_x = jnp.einsum("zyx,kx->zyk", forcing_field, table_x, precision=HIGH)
    along_yf = jnp.einsum("zyk,cy->zck", along_x, table_y, precision=HIGH)
    forcing = jnp.einsum(
        "zbk,cz->bck",
        lax.all_to_all(along_yf, "pencil", split_axis=1, concat_axis=0, tiled=True),
        table_z,
        precision=HIGH,
    )
    ky_start = lax.axis_index("pencil") * rows_y
    advanced = advance_modes(modes, earlier, forcing, extent, ky_start, size_y, size_z)
    return (field[None], advanced[None])


def solution(mesh):
    return jax.shard_map(
        local,
        mesh=mesh,
        in_specs=(P("dom", "pencil", None, None), P("dom", "pencil", None, None), P("dom")),
        out_specs=(P("dom", "pencil", None, None), P("dom", "pencil", None, None)),
        check_vma=False,
    )
```

profile of v0, /device:TPU:200, one launch (start us, length us, event | category | flops | bytes accessed | tf_op | source)
XLA Modules:
  0.0 113.1 jit_solution(10707885169397888579)
XLA Ops:
  0.7 7.0 %convolution_bitcast_fusion.3 = f32[4,512,128]{2,1,0:T(8,128)S(1)} fusion(f32[1,4,512,128]{3,2,1,0:T(8,128)} %param.3, s32[512]{0:T(512)S(1)} %multiply_add_fusion.3, f32[512]{0:T(512)S(1)} %fusion.124, pred[512]{0:T(512)(128)(4,1)S(1)} %iota_compare_fusion.2), kind=kOutput, calls=%fused_computation.14 | convolution fusion | flops 1615069184 | bytes 2101760 | tf_op jit(solution)/shard_map/bck,cz->bzk/dot_general | solution.py:70
  7.7 1.6 %copy.23 = f32[4,512,128]{2,0,1:T(4,128)} copy(f32[4,512,128]{2,1,0:T(8,128)S(1)} %convolution_bitcast_fusion.3) | data formatting | bytes 2097152 | tf_op jit(solution)/shard_map/bck,cz->bzk/transpose | solution.py:70
  9.4 10.2 %all-to-all-start = ((f32[4,512,128]{2,0,1:T(4,128)}), f32[4,512,128]{2,0,1:T(4,128)S(1)}, u32[]{:S(2)}, u32[]{:S(2)}) async-start(f32[4,512,128]{2,0,1:T(4,128)} %copy.23), calls=%async_computation | async-start | bytes 2097152 | tf_op jit(solution)/shard_map/all_to_all | solution.py:73
  20.4 27.6 %all-to-all-done = f32[4,512,128]{2,0,1:T(4,128)S(1)} async-done(((f32[4,512,128]{2,0,1:T(4,128)}), f32[4,512,128]{2,0,1:T(4,128)S(1)}, u32[]{:S(2)}, u32[]{:S(2)}) %all-to-all-start) | async-done | bytes 1048608 | tf_op jit(solution)/shard_map/all_to_all | solution.py:73
  48.1 0.1 copy.24
  48.1 0.1 copy.25
  48.3 1.5 %convolution_bitcast_fusion.2 = f32[16,128,128]{2,1,0:T(8,128)S(1)} fusion(f32[128,16,128]{2,1,0:T(8,128)S(1)} %bitcast.73, s32[128]{0:T(128)S(1)} %multiply_add_fusion.4, f32[128]{0:T(128)S(1)} %compare_select_fusion.1, pred[128]{0:T(512)(128)(4,1)S(1)} %iota_compare_fusion.3), kind=kOutput, calls=%fused_computation.13 | convolution fusion | flops 402931712 | bytes 2098304 | tf_op jit(solution)/shard_map/yzk,ya->zak/dot_general | solution.py:71
  49.8 1.9 %fusion.79 = f32[16,128,128]{1,2,0:T(8,128)S(1)} fusion(f32[16,128,128]{2,1,0:T(8,128)S(1)} %convolution_bitcast_fusion.2, f32[]{:T(128)S(6)} %mul.200, s32[]{:T(128)S(6)} %select_n.92, f32[128]{0:T(128)S(1)} %compare_select_fusion, s32[128]{0:T(128)S(1)} %multiply_add_fusion.4, pred[]{:T(512)S(6)} %lt.64, pred[128]{0:T(512)(128)(4,1)S(1)} %iota_compare_fusion.4), kind=kOutput, calls=%fused_computation.99 | convolution fusion | flops 402882560 | bytes 2098313 | tf_op jit(solution)/shard_map/zyk,kx->zyx/dot_general | solution.py:77
  51.8 1.9 %collective-permute-start.1 = (f32[3,16,128]{2,0,1:T(4,128)S(1)}, f32[3,16,128]{2,0,1:T(4,128)S(1)}, u32[]{:S(2)}, u32[]{:S(2)}) collective-permute-start(f32[3,16,128]{2,0,1:T(4,128)S(1)} %get-tuple-element.11), channel_id=1, source_target_pairs={{32,0},{64,32},{96,64},{128,96},{160,128},{192,160},{224,192},{256... | collective-permute-start | bytes 73736 | tf_op jit(solution)/shard_map/ppermute | solution.py:16
  53.7 0.1 pad_add_fusion
  53.8 2.6 %collective-permute-start = (f32[3,16,128]{2,0,1:T(4,128)S(1)}, f32[3,16,128]{2,0,1:T(4,128)S(1)}, u32[]{:S(2)}, u32[]{:S(2)}) collective-permute-start(f32[3,16,128]{2,0,1:T(4,128)S(1)} %rev.3), channel_id=1, source_target_pairs={{0,32},{32,64},{64,96},{96,128},{128,160},{160,192},{192,224},{224... | collective-permute-start | bytes 73736 | tf_op jit(solution)/shard_map/ppermute | solution.py:16
  56.4 0.0 collective-permute-done.1
  56.5 2.6 %collective-permute-done = f32[3,16,128]{2,0,1:T(4,128)S(1)} collective-permute-done((f32[3,16,128]{2,0,1:T(4,128)S(1)}, f32[3,16,128]{2,0,1:T(4,128)S(1)}, u32[]{:S(2)}, u32[]{:S(2)}) %collective-permute-start) | collective-permute-done | bytes 24608 | tf_op jit(solution)/shard_map/ppermute | solution.py:16
  59.1 0.1 maximum_multiply_fusion
  59.2 1.0 fusion.63
  60.2 1.9 %fusion.77 = f32[16,128,128]{2,1,0:T(8,128)S(1)} fusion(f32[16,128,128]{2,1,0:T(8,128)S(1)} %fusion.63, f32[]{:T(128)S(6)} %mul.200, s32[]{:T(128)S(6)} %select_n.92, f32[128]{0:T(128)S(1)} %compare_select_fusion, s32[128]{0:T(128)S(1)} %multiply_add_fusion.4, pred[]{:T(512)S(6)} %lt.64, pred[128]{0:T(512)(128)(4,1)S(1)} %iota_compare_fusion.4), kind=kOutput, calls=%fused_computation.98 | convolution fusion | flops 402882560 | bytes 2098313 | tf_op jit(solution)/shard_map/zyx,kx->zyk/dot_general | solution.py:91
  62.1 1.3 %convolution_bitcast_fusion.1 = f32[16,128,128]{2,1,0:T(8,128)S(1)} fusion(f32[16,128,128]{2,1,0:T(8,128)S(1)} %fusion.77, s32[128]{0:T(128)S(1)} %multiply_add_fusion.4, f32[128]{0:T(128)S(1)} %compare_select_fusion.1, pred[128]{0:T(512)(128)(4,1)S(1)} %iota_compare_fusion.3), kind=kOutput, calls=%fused_computation.12 | convolution fusion | flops 402931712 | bytes 2098304 | tf_op jit(solution)/shard_map/zyk,cy->zck/dot_general | solution.py:92
  63.4 1.6 %copy.29 = f32[16,128,128]{2,0,1:T(8,128)} copy(f32[16,128,128]{2,1,0:T(8,128)S(1)} %convolution_bitcast_fusion.1) | data formatting | bytes 2097152 | tf_op jit(solution)/shard_map/zyk,cy->zck/transpose | solution.py:92
  65.0 5.2 %all-to-all-start.1 = ((f32[16,128,128]{2,0,1:T(8,128)}), f32[16,128,128]{2,0,1:T(8,128)S(1)}, u32[]{:S(2)}, u32[]{:S(2)}) async-start(f32[16,128,128]{2,0,1:T(8,128)} %copy.29), calls=%async_computation.1 | async-start | bytes 2097152 | tf_op jit(solution)/shard_map/all_to_all | solution.py:95
  70.2 1.3 %copy.31 = f32[1,16,128,128]{3,2,1,0:T(8,128)} copy(f32[1,16,128,128]{2,3,1,0:T(8,128)S(1)} %bitcast.72) | data formatting | bytes 2097152
  71.5 28.3 %all-to-all-done.1 = f32[16,128,128]{2,0,1:T(8,128)S(1)} async-done(((f32[16,128,128]{2,0,1:T(8,128)}), f32[16,128,128]{2,0,1:T(8,128)S(1)}, u32[]{:S(2)}, u32[]{:S(2)}) %all-to-all-start.1) | async-done | bytes 1048608 | tf_op jit(solution)/shard_map/all_to_all | solution.py:95
  99.8 0.0 copy-start
  99.8 0.0 copy-start.1
  99.8 0.1 copy.30
  99.9 1.1 copy-done
  101.0 0.3 copy-done.1
  101.3 11.8 %fusion.3 = f32[1,4,512,128]{3,2,1,0:T(8,128)} fusion(f32[512,4,128]{2,0,1:T(8,128)S(1)} %bitcast.76, f32[1,4,512,128]{3,2,1,0:T(8,128)S(1)} %copy-done.1, f32[1,4,512,128]{3,2,1,0:T(8,128)S(1)} %copy-done, f32[512]{0:T(512)S(1)} %multiply_multiply_fusion.4, f32[4]{0:T(128)S(1)} %multiply_multiply_fusion.5, f32[128]{0:T(128)S(1)} %divide_multiply_fusion, ...), kind=kOutput, calls=%fused_computation.16 | convolution fusion | flops 1626865664 | bytes 4201616 | tf_op jit(solution)/shard_map/zbk,cz->bck/dot_general | solution.py:93
  (19 shorter events, 0.2 us)
Async XLA Ops:
  9.4 38.7 %all-to-all-start = ((f32[4,512,128]{2,0,1:T(4,128)}), f32[4,512,128]{2,0,1:T(4,128)S(1)}, u32[]{:S(2)}, u32[]{:S(2)}) async-start(f32[4,512,128]{2,0,1:T(4,128)} %copy.23), calls=%async_computation | async-start | bytes 2097152 | tf_op jit(solution)/shard_map/all_to_all | solution.py:73
  51.8 4.7 %collective-permute-start.1 = (f32[3,16,128]{2,0,1:T(4,128)S(1)}, f32[3,16,128]{2,0,1:T(4,128)S(1)}, u32[]{:S(2)}, u32[]{:S(2)}) collective-permute-start(f32[3,16,128]{2,0,1:T(4,128)S(1)} %get-tuple-element.11), channel_id=1, source_target_pairs={{32,0},{64,32},{96,64},{128,96},{160,128},{192,160},{224,192},{256... | collective-permute-start | bytes 73736 | tf_op jit(solution)/shard_map/ppermute | solution.py:16
  53.8 5.2 %collective-permute-start = (f32[3,16,128]{2,0,1:T(4,128)S(1)}, f32[3,16,128]{2,0,1:T(4,128)S(1)}, u32[]{:S(2)}, u32[]{:S(2)}) collective-permute-start(f32[3,16,128]{2,0,1:T(4,128)S(1)} %rev.3), channel_id=1, source_target_pairs={{0,32},{32,64},{64,96},{96,128},{128,160},{160,192},{192,224},{224... | collective-permute-start | bytes 73736 | tf_op jit(solution)/shard_map/ppermute | solution.py:16
  65.0 34.8 %all-to-all-start.1 = ((f32[16,128,128]{2,0,1:T(8,128)}), f32[16,128,128]{2,0,1:T(8,128)S(1)}, u32[]{:S(2)}, u32[]{:S(2)}) async-start(f32[16,128,128]{2,0,1:T(8,128)} %copy.29), calls=%async_computation.1 | async-start | bytes 2097152 | tf_op jit(solution)/shard_map/all_to_all | solution.py:95
  99.8 1.2 %copy-start = (f32[1,4,512,128]{3,2,1,0:T(8,128)S(1)}, f32[1,4,512,128]{3,2,1,0:T(8,128)}, u32[]{:S(2)}) copy-start(f32[1,4,512,128]{3,2,1,0:T(8,128)} %param.3) | copy-start | bytes 3145732
  99.8 1.5 %copy-start.1 = (f32[1,4,512,128]{3,2,1,0:T(8,128)S(1)}, f32[1,4,512,128]{3,2,1,0:T(8,128)}, u32[]{:S(2)}) copy-start(f32[1,4,512,128]{3,2,1,0:T(8,128)} %param.4) | copy-start | bytes 3145732
where the time goes:
time: 114 us; the launch traced here: 113 us
  waiting for transfers between devices  58.5 us (51%)
  matrix products  26.5 us (23%)
  starting transfers between devices  19.9 us (17%)
  local copies, waits for them, and re-layouts  6.34 us (6%)
  between operations  1.7 us (1%)
    all_to_all x1, waiting for transfers between devices, local(): lax.all_to_all(along_yf, 'pencil', split_axis=1, concat_axis=0, tiled=True)  28.3 us
    all_to_all x1, waiting for transfers between devices, local(): lax.all_to_all(along_z, 'pencil', split_axis=1, concat_axis=0, tiled=True)  27.6 us
    dot_general x1, matrix products, local(): jnp.einsum('zbk,cz->bck', lax.all_to_all(along_yf, 'pencil', split_axis=1...  11.8 us
    all_to_all x1, starting transfers between devices, local(): lax.all_to_all(along_z, 'pencil', split_axis=1, concat_axis=0, tiled=True)  10.2 us
    dot_general x1, matrix products, local(): along_z = jnp.einsum('bck,cz->bzk', modes, table_z, precision=HIGH)  7.04 us
    all_to_all x1, starting transfers between devices, local(): lax.all_to_all(along_yf, 'pencil', split_axis=1, concat_axis=0, tiled=True)  5.19 us
    ppermute x2, starting transfers between devices, from_behind(): return lax.ppermute(block, axis, route)  4.51 us
    unnamed x5, local copies, waits for them, and re-layouts  2.75 us
  transfers between devices with their start and end apart: 4, of which 3 were waited for; matrix products, arithmetic and copies ran while one was open for 1% of the time, Pallas kernels for 0%

commit v1 on v0

--- a/solution.py
+++ b/solution.py
@@ -8,6 +8,7 @@
 COEF_TWO = -0.15
 COEF_THREE = 1.0 / 90.0
 STEP_DT = 0.5
+SINC_SERIES = (1.0, -1.0 / 6, 1.0 / 120, -1.0 / 5040, 1.0 / 362880, -1.0 / 39916800, 1.0 / 6227020800, -1.0 / 1307674368000)
 
 
 def from_behind(block, axis, distance):
@@ -46,12 +47,27 @@
     mode_z = lax.broadcasted_iota(jnp.int32, shape, 1).astype(jnp.float32)
     mode_x_int = lax.broadcasted_iota(jnp.int32, shape, 2)
     mode_x = mode_x_int.astype(jnp.float32)
-    frequency = jnp.pi * jnp.sqrt(
+    half = jnp.pi * STEP_DT / 2.0
+    square = half * half * (
         (mode_x / extent.astype(jnp.float32)) ** 2 + (mode_y / size_y) ** 2 + (mode_z / size_z) ** 2
     )
-    gain_force = STEP_DT * STEP_DT * jnp.sinc(frequency * STEP_DT / (2.0 * jnp.pi)) ** 2
-    advanced = 2.0 * jnp.cos(frequency * STEP_DT) * modes - earlier + gain_force * forcing
+    series = jnp.float32(SINC_SERIES[-1])
+    for term in SINC_SERIES[-2::-1]:
+        series = series * square + jnp.float32(term)
+    gain = series * series
+    advanced = 2.0 * modes - earlier + gain * (STEP_DT * STEP_DT * forcing - 4.0 * square * modes)
     return jnp.where(mode_x_int < extent, advanced, jnp.float32(0.0))
+
+
+def face_columns(live, size):
+    offsets = jnp.arange(3, dtype=jnp.int32)
+    cells = jnp.concatenate([offsets, live - 1 - offsets])
+    mode_index = lax.broadcasted_iota(jnp.int32, (size, 6), 0)
+    phase_index = mode_index * (2 * cells[None, :] + 1) % (4 * live)
+    count = live.astype(jnp.float32)
+    radians = jnp.pi * phase_index.astype(jnp.float32) / (2.0 * count)
+    norm_factor = jnp.where(mode_index == 0, jnp.sqrt(1.0 / count), jnp.sqrt(2.0 / count))
+    return jnp.where(mode_index < live, norm_factor * jnp.cos(radians), jnp.float32(0.0))
 
 
 def local(modes_now, modes_prev, extents):
@@ -65,6 +81,7 @@
     table_z = cosine_table(size_z, size_z)
     table_y = cosine_table(size_y, size_y)
     table_x = cosine_table(extent, size_x)
+    columns = face_columns(extent, size_x)
     domain = lax.axis_index("dom")
     domains = lax.axis_size("dom")
     along_z = jnp.einsum("bck,cz->bzk", modes, table_z, precision=HIGH)
@@ -75,27 +92,14 @@
         precision=HIGH,
     )
     field = jnp.einsum("zyk,kx->zyx", along_y, table_x, precision=HIGH)
-    lower_rim = jnp.moveaxis(field[:, :, 0:3], 2, 0)
-    upper_block = lax.dynamic_slice_in_dim(field, extent - 3, 3, axis=2)
-    upper_rim = jnp.moveaxis(upper_block, 2, 0)[::-1]
+    rims = jnp.einsum("kl,bck->lbc", columns, modes, precision=HIGH)
+    lower_rim, upper_rim = rims[:3], rims[3:]
     from_lower = from_behind(upper_rim, "dom", 1)
     from_upper = from_behind(lower_rim, "dom", -1)
     lower_force = face_forcing(lower_rim, from_lower) * (domain > 0).astype(jnp.float32)
     upper_force = face_forcing(upper_rim, from_upper) * (domain < domains - 1).astype(jnp.float32)
     layers = jnp.concatenate([lower_force, upper_force], axis=0)
-    offsets = jnp.arange(3, dtype=jnp.int32)
-    positions = jnp.concatenate([offsets, extent - 1 - offsets])
-    columns = lax.broadcasted_iota(jnp.int32, (6, size_x), 1)
-    onehot = (columns == positions[:, None]).astype(jnp.float32)
-    forcing_field = jnp.einsum("lzy,lx->zyx", layers, onehot, precision=HIGH)
-    along_x = jnp.einsum("zyx,kx->zyk", forcing_field, table_x, precision=HIGH)
-    along_yf = jnp.einsum("zyk,cy->zck", along_x, table_y, precision=HIGH)
-    forcing = jnp.einsum(
-        "zbk,cz->bck",
-        lax.all_to_all(along_yf, "pencil", split_axis=1, concat_axis=0, tiled=True),
-        table_z,
-        precision=HIGH,
-    )
+    forcing = jnp.einsum("lbc,kl->bck", layers, columns, precision=HIGH)
     ky_start = lax.axis_index("pencil") * rows_y
     advanced = advance_modes(modes, earlier, forcing, extent, ky_start, size_y, size_z)
     return (field[None], advanced[None])

time: 114 us -> 53.1 us (0.47)
  waiting for transfers between devices: 58.5 us -> 16.5 us
  matrix products: 26.5 us -> 16.3 us
  local copies, waits for them, and re-layouts: 6.34 us -> 1.88 us
  starting transfers between devices: 19.9 us -> 16 us
    all_to_all x1 -> x0, waiting for transfers between devices: 28.3 us -> none  [local(): lax.all_to_all(along_yf, 'pencil', split_axis=1, concat_axis=0, tiled=True)]
    all_to_all x1, waiting for transfers between devices: 27.6 us -> 14.2 us  [local(): lax.all_to_all(along_z, 'pencil', split_axis=1, concat_axis=0, tiled=True)]
    dot_general x4 -> x2, matrix products: 16 us -> 4.87 us  [the longest x1 3.71 us: local(): forcing = jnp.einsum('lbc,kl->bck', layers, columns, precision=HIGH)]
    all_to_all x1 -> x0, starting transfers between devices: 5.19 us -> none  [local(): lax.all_to_all(along_yf, 'pencil', split_axis=1, concat_axis=0, tiled=True)]
    unnamed x5 -> x4, local copies, waits for them, and re-layouts: 2.75 us -> 0.01 us
    transpose x2 -> x0, local copies, waits for them, and re-layouts: 1.61 us -> none  [the longest x1 1.58 us: local(): along_yf = jnp.einsum('zyk,cy->zck', along_x, table_y, precision=HIGH)]
    ppermute x2, starting transfers between devices: 4.51 us -> 5.74 us  [from_behind(): return lax.ppermute(block, axis, route)]
  transfers between devices with their start and end apart: 4 -> 3, of which waited for: 3 -> 2; matrix products, arithmetic and copies ran while one was open for 1% -> 10% of each run, Pallas kernels for 0% -> 0%
where the time goes in v1:
time: 53.1 us; the launch traced here: 52.8 us
  waiting for transfers between devices  16.5 us (31%)
  matrix products  16.3 us (31%)
  starting transfers between devices  16 us (30%)
  local copies, waits for them, and re-layouts  1.88 us (4%)
  between operations  1.76 us (3%)
    all_to_all x1, waiting for transfers between devices, local(): lax.all_to_all(along_z, 'pencil', split_axis=1, concat_axis=0, tiled=True)  14.2 us
    all_to_all x1, starting transfers between devices, local(): lax.all_to_all(along_z, 'pencil', split_axis=1, concat_axis=0, tiled=True)  10.3 us
    dot_general x1, matrix products, local(): along_z = jnp.einsum('bck,cz->bzk', modes, table_z, precision=HIGH)  7.05 us
    ppermute x2, starting transfers between devices, from_behind(): return lax.ppermute(block, axis, route)  5.74 us
    dot_general x1, matrix products, local(): forcing = jnp.einsum('lbc,kl->bck', layers, columns, precision=HIGH)  3.71 us
    dot_general x1, matrix products, local(): field = jnp.einsum('zyk,kx->zyx', along_y, table_x, precision=HIGH)  2.86 us
    ppermute x2, waiting for transfers between devices, from_behind(): return lax.ppermute(block, axis, route)  2.37 us
    transpose x1, local copies, waits for them, and re-layouts, local(): along_z = jnp.einsum('bck,cz->bzk', modes, table_z, precision=HIGH)  1.65 us
  transfers between devices with their start and end apart: 3, of which 2 were waited for; matrix products, arithmetic and copies ran while one was open for 10% of the time, Pallas kernels for 0%

profile of v1, /device:TPU:200, one launch (start us, length us, event | category | flops | bytes accessed | tf_op | source)
XLA Modules:
  0.0 52.8 jit_solution(15734728785288409558)
XLA Ops:
  0.7 7.0 %convolution_bitcast_fusion.2 = f32[4,512,128]{2,1,0:T(8,128)S(1)} fusion(f32[1,4,512,128]{3,2,1,0:T(8,128)} %param.3, s32[512]{0:T(512)S(1)} %multiply_add_fusion.2, f32[512]{0:T(512)S(1)} %fusion.117, pred[512]{0:T(512)(128)(4,1)S(1)} %iota_compare_fusion.1), kind=kOutput, calls=%fused_computation.7 | convolution fusion | flops 1615069184 | bytes 2101760 | tf_op jit(solution)/shard_map/bck,cz->bzk/dot_general | solution.py:87
  7.7 1.6 %copy.9 = f32[4,512,128]{2,0,1:T(4,128)} copy(f32[4,512,128]{2,1,0:T(8,128)S(1)} %convolution_bitcast_fusion.2) | data formatting | bytes 2097152 | tf_op jit(solution)/shard_map/bck,cz->bzk/transpose | solution.py:87
  9.4 0.0 copy-start
  9.4 10.3 %all-to-all-start = ((f32[4,512,128]{2,0,1:T(4,128)}), f32[4,512,128]{2,0,1:T(4,128)S(1)}, u32[]{:S(2)}, u32[]{:S(2)}) async-start(f32[4,512,128]{2,0,1:T(4,128)} %copy.9), calls=%async_computation | async-start | bytes 2097152 | tf_op jit(solution)/shard_map/all_to_all | solution.py:90
  19.7 0.0 copy-start.1
  20.6 0.1 fusion.122
  20.7 0.0 copy-done
  20.7 1.2 %fusion.13 = f32[6,4,512]{2,0,1:T(8,128)S(1)} fusion(f32[1,4,512,128]{3,2,1,0:T(8,128)S(1)} %copy-done, f32[]{:T(128)S(6)} %mul.200, s32[]{:T(128)S(6)} %select_n.68, s32[6]{0:T(128)S(1)} %fusion.122, f32[128]{0:T(128)S(1)} %compare_select_fusion, pred[]{:T(512)S(6)} %lt.62, pred[128]{0:T(512)(128)(4,1)S(1)} %iota_compare_fusion.3), kind=kOutput, calls=%fused_computation.21 | convolution fusion | flops 18884352 | bytes 1098401 | tf_op jit(solution)/shard_map/kl,bck->lbc/dot_general | solution.py:95
  21.9 1.9 %collective-permute-start = (f32[3,4,512]{2,0,1:T(4,128)S(1)}, f32[3,4,512]{2,0,1:T(4,128)S(1)}, u32[]{:S(2)}, u32[]{:S(2)}) collective-permute-start(f32[3,4,512]{2,0,1:T(4,128)S(1)} %get-tuple-element.4), channel_id=1, source_target_pairs={{0,32},{32,64},{64,96},{96,128},{128,160},{160,192},{192,224},{224... | collective-permute-start | bytes 73736 | tf_op jit(solution)/shard_map/ppermute | solution.py:17
  23.8 3.8 %collective-permute-start.1 = (f32[3,4,512]{2,0,1:T(4,128)S(1)}, f32[3,4,512]{2,0,1:T(4,128)S(1)}, u32[]{:S(2)}, u32[]{:S(2)}) collective-permute-start(f32[3,4,512]{2,0,1:T(4,128)S(1)} %get-tuple-element.5), channel_id=1, source_target_pairs={{32,0},{64,32},{96,64},{128,96},{160,128},{192,160},{224,192},{256... | collective-permute-start | bytes 73736 | tf_op jit(solution)/shard_map/ppermute | solution.py:17
  27.8 0.0 collective-permute-done
  27.8 2.4 %collective-permute-done.1 = f32[3,4,512]{2,0,1:T(4,128)S(1)} collective-permute-done((f32[3,4,512]{2,0,1:T(4,128)S(1)}, f32[3,4,512]{2,0,1:T(4,128)S(1)}, u32[]{:S(2)}, u32[]{:S(2)}) %collective-permute-start.1) | collective-permute-done | bytes 24608 | tf_op jit(solution)/shard_map/ppermute | solution.py:17
  30.2 0.1 fusion.88
  30.3 0.0 copy-done.1
  30.3 3.7 %fusion.4 = f32[1,4,512,128]{3,2,1,0:T(8,128)} fusion(f32[1,4,512,128]{3,2,1,0:T(8,128)S(1)} %copy-done.1, f32[1,4,512,128]{3,2,1,0:T(8,128)S(1)} %copy-done, f32[512]{0:T(512)S(1)} %multiply_multiply_fusion.4, f32[4]{0:T(128)S(1)} %multiply_multiply_fusion.5, f32[128]{0:T(128)S(1)} %divide_multiply_fusion, pred[128]{0:T(512)(128)(4,1)S(1)} %iota_compare_fusion.3, ...), kind=kOutput, calls=%fused_computation.11 | convolution fusion | flops 25974528 | bytes 3198129 | tf_op jit(solution)/shard_map/lbc,kl->bck/dot_general | solution.py:102
  34.0 14.2 %all-to-all-done = f32[4,512,128]{2,0,1:T(4,128)S(1)} async-done(((f32[4,512,128]{2,0,1:T(4,128)}), f32[4,512,128]{2,0,1:T(4,128)S(1)}, u32[]{:S(2)}, u32[]{:S(2)}) %all-to-all-start) | async-done | bytes 1048608 | tf_op jit(solution)/shard_map/all_to_all | solution.py:90
  48.2 0.1 copy.10
  48.3 0.1 copy.11
  48.4 1.5 %convolution_bitcast_fusion.1 = f32[16,128,128]{2,1,0:T(8,128)S(1)} fusion(f32[128,16,128]{2,1,0:T(8,128)S(1)} %bitcast.46, s32[128]{0:T(128)S(1)} %multiply_add_fusion.3, f32[128]{0:T(128)S(1)} %compare_select_fusion.1, pred[128]{0:T(512)(128)(4,1)S(1)} %iota_compare_fusion.2), kind=kOutput, calls=%fused_computation.6 | convolution fusion | flops 402931712 | bytes 2098304 | tf_op jit(solution)/shard_map/yzk,ya->zak/dot_general | solution.py:88
  49.9 2.9 %convolution_bitcast_fusion = f32[1,16,128,128]{3,2,1,0:T(8,128)} fusion(f32[16,128,128]{2,1,0:T(8,128)S(1)} %convolution_bitcast_fusion.1, f32[]{:T(128)S(6)} %mul.200, s32[]{:T(128)S(6)} %select_n.68, f32[128]{0:T(128)S(1)} %compare_select_fusion, s32[128]{0:T(128)S(1)} %multiply_add_fusion.3, pred[]{:T(512)S(6)} %lt.62, ...), kind=kOutput, calls=%fused_computation.5 | convolution fusion | flops 402882560 | bytes 2098313 | tf_op jit(solution)/shard_map/zyk,kx->zyx/dot_general | solution.py:94
  (17 shorter events, 0.2 us)
Async XLA Ops:
  9.4 11.4 %copy-start = (f32[1,4,512,128]{3,2,1,0:T(8,128)S(1)}, f32[1,4,512,128]{3,2,1,0:T(8,128)}, u32[]{:S(2)}) copy-start(f32[1,4,512,128]{3,2,1,0:T(8,128)} %param.3) | copy-start | bytes 3145732
  9.4 38.8 %all-to-all-start = ((f32[4,512,128]{2,0,1:T(4,128)}), f32[4,512,128]{2,0,1:T(4,128)S(1)}, u32[]{:S(2)}, u32[]{:S(2)}) async-start(f32[4,512,128]{2,0,1:T(4,128)} %copy.9), calls=%async_computation | async-start | bytes 2097152 | tf_op jit(solution)/shard_map/all_to_all | solution.py:90
  19.7 10.6 %copy-start.1 = (f32[1,4,512,128]{3,2,1,0:T(8,128)S(1)}, f32[1,4,512,128]{3,2,1,0:T(8,128)}, u32[]{:S(2)}) copy-start(f32[1,4,512,128]{3,2,1,0:T(8,128)} %param.4) | copy-start | bytes 3145732
  21.9 5.8 %collective-permute-start = (f32[3,4,512]{2,0,1:T(4,128)S(1)}, f32[3,4,512]{2,0,1:T(4,128)S(1)}, u32[]{:S(2)}, u32[]{:S(2)}) collective-permute-start(f32[3,4,512]{2,0,1:T(4,128)S(1)} %get-tuple-element.4), channel_id=1, source_target_pairs={{0,32},{32,64},{64,96},{96,128},{128,160},{160,192},{192,224},{224... | collective-permute-start | bytes 73736 | tf_op jit(solution)/shard_map/ppermute | solution.py:17
  23.8 6.3 %collective-permute-start.1 = (f32[3,4,512]{2,0,1:T(4,128)S(1)}, f32[3,4,512]{2,0,1:T(4,128)S(1)}, u32[]{:S(2)}, u32[]{:S(2)}) collective-permute-start(f32[3,4,512]{2,0,1:T(4,128)S(1)} %get-tuple-element.5), channel_id=1, source_target_pairs={{32,0},{64,32},{96,64},{128,96},{160,128},{192,160},{224,192},{256... | collective-permute-start | bytes 73736 | tf_op jit(solution)/shard_map/ppermute | solution.py:17

commit v2 on v0

v2 whole, which is shorter than its diff:
```python
import functools

import jax
import jax.numpy as jnp
import numpy as np
from jax import lax
from jax.experimental import pallas as pl
from jax.experimental.pallas import tpu as pltpu
from jax.sharding import PartitionSpec as P

COEF_ONE = 1.5
COEF_TWO = -0.15
COEF_THREE = 1.0 / 90.0
STEP_DT = 0.5
SINC_SERIES = (1.0, -1.0 / 6, 1.0 / 120, -1.0 / 5040, 1.0 / 362880, -1.0 / 39916800, 1.0 / 6227020800, -1.0 / 1307674368000)
MESH = pl.DeviceIdType.MESH
BF16 = jnp.bfloat16
F32 = jnp.float32

NX, NY = 4, 8
NP = NX * NY
KY = 4
ZB = 16
GX, GY, GZ = 128, 128, 512
ROWS = KY * ZB
PAIRS = ((1, 7), (2, 6), (3, 5), (4, 0))


def split(value):
    high = value.astype(BF16)
    return high, (value - high.astype(F32)).astype(BF16)


def dot3(a, b, dims=(((1,), (0,)), ((), ()))):
    mul = functools.partial(lax.dot_general, dimension_numbers=dims, preferred_element_type=F32)
    return mul(a[0], b[0]) + (mul(a[0], b[1]) + mul(a[1], b[0]))


def cosine(phase, count):
    turns = jnp.floor(phase / (4.0 * count))
    phase = phase - turns * (4.0 * count)
    angle = (jnp.abs(phase - 2.0 * count) - count) / count * (jnp.pi / 2.0)
    square = angle * angle
    series = jnp.full_like(square, SINC_SERIES[-1])
    for term in SINC_SERIES[-2::-1]:
        series = series * square + term
    return angle * series


def table(mode, cell, count, inside):
    scale = jnp.sqrt(jnp.where(mode == 0.0, 1.0, 2.0) / count)
    return jnp.where(inside, scale * cosine(mode * (2.0 * cell + 1.0), count), 0.0)


def exchange_kernel(
    modes_hbm, prev_hbm, extent_ref, tzh_hbm, tzl_hbm, recv, next_hbm,
    modes, prev, tzh, tzl, high, low, send, rims, rim_out, from_lower, from_upper, nxt,
    in_sem, send_sem, recv_sem, rim_sem, out_sem,
):
    dom = lax.axis_index("dom")
    doms = lax.axis_size("dom")
    me = lax.axis_index("pencil")
    my_x, my_y = me // NY, me % NY
    above, below = (dom + 1) % doms, (dom + doms - 1) % doms

    loads = [
        pltpu.make_async_copy(modes_hbm, modes, in_sem.at[0]),
        pltpu.make_async_copy(tzh_hbm, tzh, in_sem.at[1]),
        pltpu.make_async_copy(tzl_hbm, tzl, in_sem.at[2]),
        pltpu.make_async_copy(prev_hbm, prev, in_sem.at[3]),
    ]
    for load in loads:
        load.start()

    barrier = pltpu.get_barrier_semaphore()

    def signal(i, carry):
        pl.semaphore_signal(barrier, inc=1, device_id={"pencil": (me + i) % NP}, device_id_type=MESH)
        return carry

    lax.fori_loop(1, NP, signal, 0)
    for other in (above, below):
        pl.semaphore_signal(barrier, inc=1, device_id={"dom": other}, device_id_type=MESH)

    count = jnp.full((8, GX), extent_ref[0, 0]).astype(F32)
    count_x = jnp.concatenate([count] * (GX // 8), axis=0)
    mode = lax.broadcasted_iota(jnp.int32, (GX, GX), 0).astype(F32)
    cell = lax.broadcasted_iota(jnp.int32, (GX, GX), 1).astype(F32)
    table_x = split(table(mode, cell, count_x, (mode < count_x) & (cell < count_x)))

    row = lax.broadcasted_iota(jnp.int32, (8, GX), 0).astype(F32)
    lane = lax.broadcasted_iota(jnp.int32, (8, GX), 1).astype(F32)
    upper = row >= 3.0
    layer = jnp.where(upper, row - 3.0, row)
    live = (lane < count) & (row < 6.0)

    def face(offset, is_upper):
        return table(lane, jnp.where(is_upper, count - 1.0 - offset, offset), count, live)

    own = face(layer, upper)
    swapped = face(layer, jnp.logical_not(upper))
    weights = ((COEF_ONE, COEF_TWO, COEF_THREE), (COEF_TWO, COEF_THREE, 0.0), (COEF_THREE, 0.0, 0.0))
    spread = jnp.zeros((8, GX), F32)
    for offset in range(3):
        factor = jnp.zeros((8, GX), F32)
        for m in range(3):
            factor = jnp.where(layer == float(m), weights[offset][m], factor)
        spread += factor * face(jnp.full((8, GX), float(offset)), upper)
    has_lower = jnp.where(dom > 0, 1.0, 0.0)
    has_upper = jnp.where(dom < doms - 1, 1.0, 0.0)
    spread = spread * jnp.where(upper, has_upper, has_lower)

    loads[0].wait()
    for ky in range(KY):
        h, l = split(modes[ky])
        high[:, ky * GX : (ky + 1) * GX] = h
        low[:, ky * GX : (ky + 1) * GX] = l
    loads[1].wait()
    loads[2].wait()

    def make_pair(chunk):
        starts = [((my_y + dy) % NY) for dy in PAIRS[chunk]]
        th = jnp.concatenate([tzh[y] for y in starts], axis=0)
        tl = jnp.concatenate([tzl[y] for y in starts], axis=0)
        along_z = dot3((th, tl), (high[...], low[...]))
        along_z = jnp.concatenate([along_z[:, ky * GX : (ky + 1) * GX] for ky in range(KY)], axis=0)
        along_x = dot3(split(along_z), table_x)
        for ky in range(KY):
            for half in range(2):
                for x in range(NX):
                    begin = ky * 2 * NX * ZB + (half * NX + x) * ZB
                    send[(2 * chunk + half) * NX + x, pl.ds(ky, ZB, stride=KY), :] = along_x[begin : begin + ZB]

    def transfer(slot_half, dx, dy):
        x, y = (my_x + dx) % NX, (my_y + dy) % NY
        index = dx * NY + dy
        return pltpu.make_async_remote_copy(
            src_ref=send.at[slot_half * NX + x],
            dst_ref=recv.at[me],
            send_sem=send_sem.at[index],
            recv_sem=recv_sem.at[index],
            device_id={"pencil": x * NY + y},
            device_id_type=MESH,
        )

    keep = pltpu.make_async_copy(send.at[7 * NX + my_x], recv.at[me], send_sem.at[0])

    def send_pair(chunk):
        for half in range(2):
            dy = PAIRS[chunk][half]
            first = 1 if dy == 0 else 0

            def go(dx, carry):
                transfer(2 * chunk + half, dx, dy).start()
                return carry

            lax.fori_loop(first, NX, go, 0)
            if dy == 0:
                keep.start()

    make_pair(0)
    pl.semaphore_wait(barrier, NP - 1 + 2)
    send_pair(0)

    columns = split(jnp.concatenate([own, swapped], axis=0))
    nt = (((1,), (1,)), ((), ()))
    for ky in range(KY):
        lanes = slice(ky * GX, (ky + 1) * GX)
        both = dot3(columns, (high[:, lanes], low[:, lanes]), nt)
        rims[ky] = both[:8]
        rim_out[ky] = both[8:]
    to_above = pltpu.make_async_remote_copy(
        src_ref=rim_out, dst_ref=from_lower, send_sem=rim_sem.at[0], recv_sem=rim_sem.at[1],
        device_id={"dom": above}, device_id_type=MESH,
    )
    to_below = pltpu.make_async_remote_copy(
        src_ref=rim_out, dst_ref=from_upper, send_sem=rim_sem.at[2], recv_sem=rim_sem.at[3],
        device_id={"dom": below}, device_id_type=MESH,
    )
    to_above.start()
    to_below.start()

    for chunk in range(1, 4):
        make_pair(chunk)
        send_pair(chunk)

    loads[3].wait()
    to_above.wait()
    to_below.wait()
    spread_h, spread_l = split(spread)
    spread3 = jnp.concatenate([spread_h, spread_h, spread_l, jnp.zeros_like(spread_h)], axis=0)
    half_step = (np.pi * STEP_DT / 2.0) ** 2
    part = 64
    mode_x = lax.broadcasted_iota(jnp.int32, (part, GX), 1).astype(F32)
    mode_z = lax.broadcasted_iota(jnp.int32, (part, GX), 0).astype(F32)
    count_p = jnp.concatenate([count] * (part // 8), axis=0)
    square_x = (mode_x / count_p) * (mode_x / count_p) * half_step
    is_upper = lax.broadcasted_iota(jnp.int32, (8, GZ), 0) >= 3
    for ky in range(KY):
        diff = jnp.where(is_upper, from_upper[ky], from_lower[ky]) - rims[ky]
        diff_h, diff_l = split(diff)
        diff3 = jnp.concatenate(
            [diff_h.astype(F32), diff_l.astype(F32), diff_h.astype(F32), jnp.zeros_like(diff)], axis=0
        )
        forcing = jnp.dot(diff3.T.astype(BF16), spread3, preferred_element_type=F32)
        mode_y = (me * KY + ky).astype(F32)
        square_xy = square_x + mode_y * mode_y * (half_step / (GY * GY))
        for begin in range(0, GZ, part):
            zs = mode_z + float(begin)
            square = square_xy + zs * zs * (half_step / (GZ * GZ))
            series = jnp.full_like(square, SINC_SERIES[-1])
            for term in SINC_SERIES[-2::-1]:
                series = series * square + term
            now = modes[ky, begin : begin + part, :]
            old = prev[ky, begin : begin + part, :]
            force = forcing[begin : begin + part, :]
            value = 2.0 * now - old + series * series * (STEP_DT * STEP_DT * force - 4.0 * square * now)
            nxt[ky, begin : begin + part, :] = jnp.where(mode_x < count_p, value, 0.0)
    out = pltpu.make_async_copy(nxt, next_hbm, out_sem)
    out.start()

    keep.wait()
    for chunk in range(4):
        for half in range(2):
            dy = PAIRS[chunk][half]

            def done(dx, carry):
                transfer(2 * chunk + half, dx, dy).wait()
                return carry

            lax.fori_loop(1 if dy == 0 else 0, NX, done, 0)
    out.wait()


def field_kernel(recv, th, tl, nxt, field, nxt_out, sem):
    out = pltpu.make_async_copy(nxt, nxt_out, sem)
    out.start()
    for q in range(0, 8, 2):
        parts = [recv[:, 8 * i : 8 * i + 8, :].reshape(NP * 8, GX) for i in (q, q + 1)]
        value = dot3((th[...], tl[...]), split(jnp.concatenate(parts, axis=1)))
        for i in range(2):
            for z in range(2):
                field[2 * (q + i) + z] = value[z * GY : (z + 1) * GY, i * GX : (i + 1) * GX]
    out.wait()


def host_split(value):
    value = value.astype(np.float32)
    high = value.astype(BF16)
    low = (value - high.astype(np.float32)).astype(BF16)
    return high, low


def host_table(size):
    mode = np.arange(size)[:, None]
    cell = np.arange(size)[None, :]
    scale = np.where(mode == 0, np.sqrt(1.0 / size), np.sqrt(2.0 / size))
    return scale * np.cos(np.pi * (mode * (2 * cell + 1) % (4 * size)) / (2.0 * size))


def tables():
    along_z = host_table(GZ).T
    along_z = along_z.reshape(NX, NY, ZB, GZ).transpose(1, 0, 2, 3).reshape(NY, NX * ZB, GZ)
    along_y = host_table(GY)
    pair = np.zeros((2, GY, NP, 2, KY))
    for z in range(2):
        pair[z, :, :, z, :] = along_y.T.reshape(GY, NP, KY)
    return host_split(along_z), host_split(pair.reshape(2 * GY, NP * 2 * KY))


def local(modes_now, modes_prev, extents):
    (tzh, tzl), (tyh, tyl) = tables()
    any_space = pl.BlockSpec(memory_space=pl.ANY)
    vmem = pl.BlockSpec(memory_space=pltpu.VMEM)
    recv, nxt = pl.pallas_call(
        exchange_kernel,
        out_shape=(
            jax.ShapeDtypeStruct((NP, ROWS, GX), F32),
            jax.ShapeDtypeStruct((KY, GZ, GX), F32),
        ),
        in_specs=[any_space, any_space, pl.BlockSpec(memory_space=pltpu.SMEM), any_space, any_space],
        out_specs=(any_space, any_space),
        scratch_shapes=[
            pltpu.VMEM((KY, GZ, GX), F32),
            pltpu.VMEM((KY, GZ, GX), F32),
            pltpu.VMEM((NY, NX * ZB, GZ), BF16),
            pltpu.VMEM((NY, NX * ZB, GZ), BF16),
            pltpu.VMEM((GZ, KY * GX), BF16),
            pltpu.VMEM((GZ, KY * GX), BF16),
            pltpu.VMEM((NP, ROWS, GX), F32),
            pltpu.VMEM((KY, 8, GZ), F32),
            pltpu.VMEM((KY, 8, GZ), F32),
            pltpu.VMEM((KY, 8, GZ), F32),
            pltpu.VMEM((KY, 8, GZ), F32),
            pltpu.VMEM((KY, GZ, GX), F32),
            pltpu.SemaphoreType.DMA((4,)),
            pltpu.SemaphoreType.DMA((NP,)),
            pltpu.SemaphoreType.DMA((NP,)),
            pltpu.SemaphoreType.DMA((4,)),
            pltpu.SemaphoreType.DMA,
        ],
        compiler_params=pltpu.CompilerParams(
            collective_id=0, has_side_effects=True, vmem_limit_bytes=24 * 1024 * 1024
        ),
        name="exchange",
    )(modes_now[0], modes_prev[0], extents.reshape(1, 1), tzh, tzl)
    field, advanced = pl.pallas_call(
        field_kernel,
        out_shape=(
            jax.ShapeDtypeStruct((ZB, GY, GX), F32),
            jax.ShapeDtypeStruct((KY, GZ, GX), F32),
        ),
        in_specs=[vmem, vmem, vmem, any_space],
        out_specs=(vmem, any_space),
        scratch_shapes=[pltpu.SemaphoreType.DMA],
        compiler_params=pltpu.CompilerParams(vmem_limit_bytes=24 * 1024 * 1024),
        name="field",
    )(recv, tyh, tyl, nxt)
    return (field[None], advanced[None])


def solution(mesh):
    return jax.shard_map(
        local,
        mesh=mesh,
        in_specs=(P("dom", "pencil", None, None), P("dom", "pencil", None, None), P("dom")),
        out_specs=(P("dom", "pencil", None, None), P("dom", "pencil", None, None)),
        check_vma=False,
    )
```

time: 114 us -> 43.3 us (0.38)
  the two profiles are of different devices: /device:TPU:200 before, /device:TPU:201 now
where the time goes in v2:
time: 43.3 us; the launch traced here: 43 us
  Pallas kernels  37.2 us (86%)
  local copies, waits for them, and re-layouts  4.53 us (10%)
  between operations  1.31 us (3%)
    pallas_call x1, Pallas kernels, local(): pl.pallas_call(exchange_kernel, out_shape=(jax.ShapeDtypeStruct((NP, ROWS...  35.2 us
    unnamed x12, local copies, waits for them, and re-layouts  4.53 us
    pallas_call x1, Pallas kernels, local(): pl.pallas_call(field_kernel, out_shape=(jax.ShapeDtypeStruct((ZB, GY, GX)...  2.03 us

profile of v2, /device:TPU:201, one launch (start us, length us, event | category | flops | bytes accessed | tf_op | source)
XLA Modules:
  0.0 43.0 jit_solution(2333796930369525506)
XLA Ops:
  1.3 0.0 copy-start
  1.3 1.2 %copy-done = f32[1,4,512,128]{3,2,1,0:T(8,128)S(1)} copy-done((f32[1,4,512,128]{3,2,1,0:T(8,128)S(1)}, f32[1,4,512,128]{3,2,1,0:T(8,128)}, u32[]{:S(2)}) %copy-start) | copy-done | bytes 1048600
  2.5 0.0 copy-start.1
  2.5 1.2 %copy-done.1 = f32[1,4,512,128]{3,2,1,0:T(8,128)S(1)} copy-done((f32[1,4,512,128]{3,2,1,0:T(8,128)S(1)}, f32[1,4,512,128]{3,2,1,0:T(8,128)}, u32[]{:S(2)}) %copy-start.1) | copy-done | bytes 1048600
  3.7 0.0 copy-start.2
  3.7 1.0 %copy-done.2 = bf16[8,64,512]{2,1,0:T(8,128)(2,1)S(1)} copy-done((bf16[8,64,512]{2,1,0:T(8,128)(2,1)S(1)}, bf16[8,64,512]{2,1,0:T(8,128)(2,1)}, u32[]{:S(2)}) %copy-start.2) | copy-done | bytes 524312
  4.8 0.0 copy-start.3
  4.8 1.0 %copy-done.3 = bf16[8,64,512]{2,1,0:T(8,128)(2,1)S(1)} copy-done((bf16[8,64,512]{2,1,0:T(8,128)(2,1)S(1)}, bf16[8,64,512]{2,1,0:T(8,128)(2,1)}, u32[]{:S(2)}) %copy-start.3) | copy-done | bytes 524312
  5.8 0.0 copy-start.4
  5.8 0.0 copy-start.5
  5.8 35.2 %exchange.1 = (f32[32,64,128]{2,1,0:T(8,128)S(1)}, f32[4,512,128]{2,1,0:T(8,128)S(1)}) custom-call(f32[4,512,128]{2,1,0:T(8,128)S(1)} %bitcast.6, f32[4,512,128]{2,1,0:T(8,128)S(1)} %bitcast.7, s32[1,1]{1,0:T(1,128)} %bitcast.5.extent_ref, bf16[8,64,512]{2,1,0:T(8,128)(2,1)S(1)} %copy-done.3, bf16[8,64,512]{2,1,0:T(8,128)(2,1)S(1)} %copy-done.2), custom_call_target="tpu_custom_call" | custom-call | tf_op jit(solution)/shard_map/exchange/pallas_call | solution.py:275
  41.0 0.0 copy-done.4
  41.0 0.0 copy-done.5
  41.0 2.0 %field.1 = (f32[16,128,128]{2,1,0:T(8,128)}, f32[4,512,128]{2,1,0:T(8,128)}) custom-call(f32[32,64,128]{2,1,0:T(8,128)S(1)} %get-tuple-element.6.recv, bf16[256,256]{1,0:T(8,128)(2,1)S(1)} %copy-done.5, bf16[256,256]{1,0:T(8,128)(2,1)S(1)} %copy-done.4, f32[4,512,128]{2,1,0:T(8,128)S(1)} %get-tuple-element.7.nxt), custom_call_target="tpu_custom_call" | custom-call | tf_op jit(solution)/shard_map/field/pallas_call | solution.py:307
Async XLA Ops:
  1.3 1.2 %copy-start = (f32[1,4,512,128]{3,2,1,0:T(8,128)S(1)}, f32[1,4,512,128]{3,2,1,0:T(8,128)}, u32[]{:S(2)}) copy-start(f32[1,4,512,128]{3,2,1,0:T(8,128)} %param.7) | copy-start | bytes 3145732
  2.5 1.2 %copy-start.1 = (f32[1,4,512,128]{3,2,1,0:T(8,128)S(1)}, f32[1,4,512,128]{3,2,1,0:T(8,128)}, u32[]{:S(2)}) copy-start(f32[1,4,512,128]{3,2,1,0:T(8,128)} %param.8) | copy-start | bytes 3145732
  3.7 1.0 %copy-start.2 = (bf16[8,64,512]{2,1,0:T(8,128)(2,1)S(1)}, bf16[8,64,512]{2,1,0:T(8,128)(2,1)}, u32[]{:S(2)}) copy-start(bf16[8,64,512]{2,1,0:T(8,128)(2,1)} %constant.9.clone.tzl_hbm) | copy-start | bytes 1572868
  4.8 1.0 %copy-start.3 = (bf16[8,64,512]{2,1,0:T(8,128)(2,1)S(1)}, bf16[8,64,512]{2,1,0:T(8,128)(2,1)}, u32[]{:S(2)}) copy-start(bf16[8,64,512]{2,1,0:T(8,128)(2,1)} %constant.8.clone.tzh_hbm) | copy-start | bytes 1572868
  5.8 35.2 %copy-start.4 = (bf16[256,256]{1,0:T(8,128)(2,1)S(1)}, bf16[256,256]{1,0:T(8,128)(2,1)}, u32[]{:S(2)}) copy-start(bf16[256,256]{1,0:T(8,128)(2,1)} %constant.11.clone.tl) | copy-start | bytes 393220
  5.8 35.2 %copy-start.5 = (bf16[256,256]{1,0:T(8,128)(2,1)S(1)}, bf16[256,256]{1,0:T(8,128)(2,1)}, u32[]{:S(2)}) copy-start(bf16[256,256]{1,0:T(8,128)(2,1)} %constant.10.clone.th) | copy-start | bytes 393220

commit v3 on v2

--- a/solution.py
+++ b/solution.py
@@ -23,7 +23,7 @@
 ZB = 16
 GX, GY, GZ = 128, 128, 512
 ROWS = KY * ZB
-PAIRS = ((1, 7), (2, 6), (3, 5), (4, 0))
+PAIRS = ((1, 7), (0, 2), (6, 3), (5, 4))
 
 
 def split(value):
@@ -53,34 +53,35 @@
 
 
 def exchange_kernel(
-    modes_hbm, prev_hbm, extent_ref, tzh_hbm, tzl_hbm, recv, next_hbm,
-    modes, prev, tzh, tzl, high, low, send, rims, rim_out, from_lower, from_upper, nxt,
-    in_sem, send_sem, recv_sem, rim_sem, out_sem,
+    modes_hbm, prev_hbm, extent_ref, tz_hbm, recv, next_out,
+    modes, prev, tz, high, low, send, rims, rim_out, from_lower, from_upper,
+    in_sem, tz_sem, send_sem, recv_sem, rim_sem, row_up, row_down, above_in,
 ):
     dom = lax.axis_index("dom")
     doms = lax.axis_size("dom")
     me = lax.axis_index("pencil")
     my_x, my_y = me // NY, me % NY
-    above, below = (dom + 1) % doms, (dom + doms - 1) % doms
-
-    loads = [
-        pltpu.make_async_copy(modes_hbm, modes, in_sem.at[0]),
-        pltpu.make_async_copy(tzh_hbm, tzh, in_sem.at[1]),
-        pltpu.make_async_copy(tzl_hbm, tzl, in_sem.at[2]),
-        pltpu.make_async_copy(prev_hbm, prev, in_sem.at[3]),
+    y_up, y_down = my_x * NY + (my_y + 1) % NY, my_x * NY + (my_y + NY - 1) % NY
+
+    barrier = pltpu.get_barrier_semaphore()
+    row_peers = [((my_x + dx) % NX) * NY + my_y for dx in (2, 1, 3)]
+    for other in row_peers + [y_up, y_down]:
+        pl.semaphore_signal(barrier, inc=1, device_id={"pencil": other}, device_id_type=MESH)
+
+    @pl.when(dom < doms - 1)
+    def _():
+        pl.semaphore_signal(barrier, inc=1, device_id={"dom": dom + 1}, device_id_type=MESH)
+
+    load_modes = pltpu.make_async_copy(modes_hbm, modes, in_sem.at[0])
+    load_prev = pltpu.make_async_copy(prev_hbm, prev, in_sem.at[1])
+    load_tz = [
+        pltpu.make_async_copy(tz_hbm.at[(my_y + dy) % NY], tz.at[slot], tz_sem.at[slot])
+        for slot, dy in enumerate(sum(PAIRS, ()))
     ]
-    for load in loads:
+    load_modes.start()
+    for load in load_tz:
         load.start()
-
-    barrier = pltpu.get_barrier_semaphore()
-
-    def signal(i, carry):
-        pl.semaphore_signal(barrier, inc=1, device_id={"pencil": (me + i) % NP}, device_id_type=MESH)
-        return carry
-
-    lax.fori_loop(1, NP, signal, 0)
-    for other in (above, below):
-        pl.semaphore_signal(barrier, inc=1, device_id={"dom": other}, device_id_type=MESH)
+    load_prev.start()
 
     count = jnp.full((8, GX), extent_ref[0, 0]).astype(F32)
     count_x = jnp.concatenate([count] * (GX // 8), axis=0)
@@ -110,18 +111,18 @@
     has_upper = jnp.where(dom < doms - 1, 1.0, 0.0)
     spread = spread * jnp.where(upper, has_upper, has_lower)
 
-    loads[0].wait()
+    load_modes.wait()
     for ky in range(KY):
         h, l = split(modes[ky])
         high[:, ky * GX : (ky + 1) * GX] = h
         low[:, ky * GX : (ky + 1) * GX] = l
-    loads[1].wait()
-    loads[2].wait()
 
     def make_pair(chunk):
-        starts = [((my_y + dy) % NY) for dy in PAIRS[chunk]]
-        th = jnp.concatenate([tzh[y] for y in starts], axis=0)
-        tl = jnp.concatenate([tzl[y] for y in starts], axis=0)
+        slots = (2 * chunk, 2 * chunk + 1)
+        for slot in slots:
+            load_tz[slot].wait()
+        th = jnp.concatenate([tz[slot, 0] for slot in slots], axis=0)
+        tl = jnp.concatenate([tz[slot, 1] for slot in slots], axis=0)
         along_z = dot3((th, tl), (high[...], low[...]))
         along_z = jnp.concatenate([along_z[:, ky * GX : (ky + 1) * GX] for ky in range(KY)], axis=0)
         along_x = dot3(split(along_z), table_x)
@@ -129,13 +130,13 @@
             for half in range(2):
                 for x in range(NX):
                     begin = ky * 2 * NX * ZB + (half * NX + x) * ZB
-                    send[(2 * chunk + half) * NX + x, pl.ds(ky, ZB, stride=KY), :] = along_x[begin : begin + ZB]
-
-    def transfer(slot_half, dx, dy):
+                    send[slots[half] * NX + x, pl.ds(ky, ZB, stride=KY), :] = along_x[begin : begin + ZB]
+
+    def transfer(slot, dy, dx):
         x, y = (my_x + dx) % NX, (my_y + dy) % NY
         index = dx * NY + dy
         return pltpu.make_async_remote_copy(
-            src_ref=send.at[slot_half * NX + x],
+            src_ref=send.at[slot * NX + x],
             dst_ref=recv.at[me],
             send_sem=send_sem.at[index],
             recv_sem=recv_sem.at[index],
@@ -143,24 +144,47 @@
             device_id_type=MESH,
         )
 
-    keep = pltpu.make_async_copy(send.at[7 * NX + my_x], recv.at[me], send_sem.at[0])
-
-    def send_pair(chunk):
-        for half in range(2):
-            dy = PAIRS[chunk][half]
-            first = 1 if dy == 0 else 0
-
-            def go(dx, carry):
-                transfer(2 * chunk + half, dx, dy).start()
-                return carry
-
-            lax.fori_loop(first, NX, go, 0)
-            if dy == 0:
-                keep.start()
+    flat = sum(PAIRS, ())
+    keep = pltpu.make_async_copy(send.at[flat.index(0) * NX + my_x], recv.at[me], send_sem.at[0])
+
+    def send_row(dy):
+        slot = flat.index(dy)
+
+        def go(dx, carry):
+            transfer(slot, dy, dx).start()
+            return carry
+
+        lax.fori_loop(1 if dy == 0 else 0, NX, go, 0)
+        if dy == 0:
+            keep.start()
+
+    def tell(semaphore, other):
+        pl.semaphore_signal(semaphore, inc=1, device_id={"pencil": other}, device_id_type=MESH)
 
     make_pair(0)
-    pl.semaphore_wait(barrier, NP - 1 + 2)
-    send_pair(0)
+    pl.semaphore_wait(barrier, 5 + (dom + doms - 1) // doms)
+    tell(row_up.at[0], y_down)
+    tell(row_down.at[0], y_up)
+
+    @pl.when(dom > 0)
+    def _():
+        pl.semaphore_signal(above_in, inc=1, device_id={"dom": dom - 1}, device_id_type=MESH)
+
+    for step in range(4):
+        pl.semaphore_wait(row_up.at[step], 1)
+        if step < 3:
+            tell(row_up.at[step + 1], y_down)
+        send_row(step + 1)
+        if step < 3:
+            pl.semaphore_wait(row_down.at[step], 1)
+            if step < 2:
+                tell(row_down.at[step + 1], y_up)
+            send_row(NY - step - 1)
+        if step == 0:
+            make_pair(1)
+            send_row(0)
+        if step < 2:
+            make_pair(step + 2)
 
     columns = split(jnp.concatenate([own, swapped], axis=0))
     nt = (((1,), (1,)), ((), ()))
@@ -171,22 +195,42 @@
         rim_out[ky] = both[8:]
     to_above = pltpu.make_async_remote_copy(
         src_ref=rim_out, dst_ref=from_lower, send_sem=rim_sem.at[0], recv_sem=rim_sem.at[1],
-        device_id={"dom": above}, device_id_type=MESH,
+        device_id={"dom": dom + 1}, device_id_type=MESH,
     )
     to_below = pltpu.make_async_remote_copy(
         src_ref=rim_out, dst_ref=from_upper, send_sem=rim_sem.at[2], recv_sem=rim_sem.at[3],
-        device_id={"dom": below}, device_id_type=MESH,
+        device_id={"dom": dom - 1}, device_id_type=MESH,
     )
-    to_above.start()
-    to_below.start()
-
-    for chunk in range(1, 4):
-        make_pair(chunk)
-        send_pair(chunk)
-
-    loads[3].wait()
-    to_above.wait()
-    to_below.wait()
+
+    @pl.when(dom > 0)
+    def _():
+        to_below.start()
+
+    @pl.when(dom < doms - 1)
+    def _():
+        pl.semaphore_wait(above_in, 1)
+        to_above.start()
+
+    load_prev.wait()
+
+    @pl.when(dom > 0)
+    def _():
+        to_above.wait_recv()
+        to_below.wait_send()
+
+    @pl.when(dom == 0)
+    def _():
+        from_lower[...] = jnp.zeros_like(from_lower)
+
+    @pl.when(dom < doms - 1)
+    def _():
+        to_below.wait_recv()
+        to_above.wait_send()
+
+    @pl.when(dom == doms - 1)
+    def _():
+        from_upper[...] = jnp.zeros_like(from_upper)
+
     spread_h, spread_l = split(spread)
     spread3 = jnp.concatenate([spread_h, spread_h, spread_l, jnp.zeros_like(spread_h)], axis=0)
     half_step = (np.pi * STEP_DT / 2.0) ** 2
@@ -215,33 +259,33 @@
             old = prev[ky, begin : begin + part, :]
             force = forcing[begin : begin + part, :]
             value = 2.0 * now - old + series * series * (STEP_DT * STEP_DT * force - 4.0 * square * now)
-            nxt[ky, begin : begin + part, :] = jnp.where(mode_x < count_p, value, 0.0)
-    out = pltpu.make_async_copy(nxt, next_hbm, out_sem)
-    out.start()
+            next_out[ky, begin : begin + part, :] = jnp.where(mode_x < count_p, value, 0.0)
 
     keep.wait()
-    for chunk in range(4):
-        for half in range(2):
-            dy = PAIRS[chunk][half]
-
-            def done(dx, carry):
-                transfer(2 * chunk + half, dx, dy).wait()
-                return carry
-
-            lax.fori_loop(1 if dy == 0 else 0, NX, done, 0)
-    out.wait()
-
-
-def field_kernel(recv, th, tl, nxt, field, nxt_out, sem):
-    out = pltpu.make_async_copy(nxt, nxt_out, sem)
-    out.start()
-    for q in range(0, 8, 2):
-        parts = [recv[:, 8 * i : 8 * i + 8, :].reshape(NP * 8, GX) for i in (q, q + 1)]
+    for dy in flat:
+        slot = flat.index(dy)
+
+        def done(dx, carry):
+            transfer(slot, dy, dx).wait()
+            return carry
+
+        lax.fori_loop(1 if dy == 0 else 0, NX, done, 0)
+
+
+def field_kernel(recv, th, tl, nxt, field_out, nxt_out, field, sem):
+    outs = [pltpu.make_async_copy(nxt, nxt_out, sem.at[4])]
+    outs[0].start()
+    for step in range(4):
+        parts = [recv[:, 8 * q : 8 * q + 8, :].reshape(NP * 8, GX) for q in (2 * step, 2 * step + 1)]
         value = dot3((th[...], tl[...]), split(jnp.concatenate(parts, axis=1)))
         for i in range(2):
             for z in range(2):
-                field[2 * (q + i) + z] = value[z * GY : (z + 1) * GY, i * GX : (i + 1) * GX]
-    out.wait()
+                field[4 * step + 2 * i + z] = value[z * GY : (z + 1) * GY, i * GX : (i + 1) * GX]
+        part = pl.ds(4 * step, 4)
+        outs.append(pltpu.make_async_copy(field.at[part], field_out.at[part], sem.at[step]))
+        outs[-1].start()
+    for out in outs:
+        out.wait()
 
 
 def host_split(value):
@@ -270,7 +314,8 @@
 
 def local(modes_now, modes_prev, extents):
     (tzh, tzl), (tyh, tyl) = tables()
-    any_space = pl.BlockSpec(memory_space=pl.ANY)
+    tz = np.stack([tzh, tzl], axis=1)
+    hbm = pl.BlockSpec(memory_space=pltpu.HBM)
     vmem = pl.BlockSpec(memory_space=pltpu.VMEM)
     recv, nxt = pl.pallas_call(
         exchange_kernel,
@@ -278,13 +323,12 @@
             jax.ShapeDtypeStruct((NP, ROWS, GX), F32),
             jax.ShapeDtypeStruct((KY, GZ, GX), F32),
         ),
-        in_specs=[any_space, any_space, pl.BlockSpec(memory_space=pltpu.SMEM), any_space, any_space],
-        out_specs=(any_space, any_space),
+        in_specs=[hbm, hbm, pl.BlockSpec(memory_space=pltpu.SMEM), hbm],
+        out_specs=(vmem, vmem),
         scratch_shapes=[
             pltpu.VMEM((KY, GZ, GX), F32),
             pltpu.VMEM((KY, GZ, GX), F32),
-            pltpu.VMEM((NY, NX * ZB, GZ), BF16),
-            pltpu.VMEM((NY, NX * ZB, GZ), BF16),
+            pltpu.VMEM((NY, 2, NX * ZB, GZ), BF16),
             pltpu.VMEM((GZ, KY * GX), BF16),
             pltpu.VMEM((GZ, KY * GX), BF16),
             pltpu.VMEM((NP, ROWS, GX), F32),
@@ -292,27 +336,29 @@
             pltpu.VMEM((KY, 8, GZ), F32),
             pltpu.VMEM((KY, 8, GZ), F32),
             pltpu.VMEM((KY, 8, GZ), F32),
-            pltpu.VMEM((KY, GZ, GX), F32),
-            pltpu.SemaphoreType.DMA((4,)),
+            pltpu.SemaphoreType.DMA((2,)),
+            pltpu.SemaphoreType.DMA((NY,)),
             pltpu.SemaphoreType.DMA((NP,)),
             pltpu.SemaphoreType.DMA((NP,)),
             pltpu.SemaphoreType.DMA((4,)),
-            pltpu.SemaphoreType.DMA,
+            pltpu.SemaphoreType.REGULAR((4,)),
+            pltpu.SemaphoreType.REGULAR((3,)),
+            pltpu.SemaphoreType.REGULAR,
         ],
         compiler_params=pltpu.CompilerParams(
             collective_id=0, has_side_effects=True, vmem_limit_bytes=24 * 1024 * 1024
         ),
         name="exchange",
-    )(modes_now[0], modes_prev[0], extents.reshape(1, 1), tzh, tzl)
+    )(*[pltpu.with_memory_space_constraint(v, pltpu.HBM) for v in (modes_now[0], modes_prev[0])], extents.reshape(1, 1), pltpu.with_memory_space_constraint(jnp.asarray(tz), pltpu.HBM))
     field, advanced = pl.pallas_call(
         field_kernel,
         out_shape=(
             jax.ShapeDtypeStruct((ZB, GY, GX), F32),
             jax.ShapeDtypeStruct((KY, GZ, GX), F32),
         ),
-        in_specs=[vmem, vmem, vmem, any_space],
-        out_specs=(vmem, any_space),
-        scratch_shapes=[pltpu.SemaphoreType.DMA],
+        in_specs=[vmem, vmem, vmem, vmem],
+        out_specs=(hbm, hbm),
+        scratch_shapes=[pltpu.VMEM((ZB, GY, GX), F32), pltpu.SemaphoreType.DMA((5,))],
         compiler_params=pltpu.CompilerParams(vmem_limit_bytes=24 * 1024 * 1024),
         name="field",
     )(recv, tyh, tyl, nxt)

time: 43.3 us -> 38.3 us (0.88)
  the two profiles are of different devices: /device:TPU:201 before, /device:TPU:200 now
where the time goes in v3:
time: 38.3 us; the launch traced here: 38.1 us
  Pallas kernels  36.8 us (96%)
  between operations  1.32 us (3%)
    pallas_call x1, Pallas kernels, local(): pl.pallas_call(exchange_kernel, out_shape=(jax.ShapeDtypeStruct((NP, ROWS...  35.4 us
    pallas_call x1, Pallas kernels, local(): pl.pallas_call(field_kernel, out_shape=(jax.ShapeDtypeStruct((ZB, GY, GX)...  1.43 us

profile of v3, /device:TPU:200, one launch (start us, length us, event | category | flops | bytes accessed | tf_op | source)
XLA Modules:
  0.0 38.1 jit_solution(7454965234971011942)
XLA Ops:
  1.3 0.0 copy-start
  1.3 0.0 copy-start.1
  1.3 35.4 %exchange.1 = (f32[32,64,128]{2,1,0:T(8,128)S(1)}, f32[4,512,128]{2,1,0:T(8,128)S(1)}) custom-call(f32[4,512,128]{2,1,0:T(8,128)} %bitcast.6, f32[4,512,128]{2,1,0:T(8,128)} %bitcast.7, s32[1,1]{1,0:T(1,128)} %bitcast.5.extent_ref, bf16[8,2,64,512]{3,2,1,0:T(8,128)(2,1)} %constant.6.clone.tz_hbm), custom_call_target="tpu_custom_call" | custom-call | tf_op jit(solution)/shard_map/exchange/pallas_call | solution.py:320
  36.7 0.0 copy-done
  36.7 0.0 copy-done.1
  36.7 1.4 %field.1 = (f32[16,128,128]{2,1,0:T(8,128)}, f32[4,512,128]{2,1,0:T(8,128)}) custom-call(f32[32,64,128]{2,1,0:T(8,128)S(1)} %get-tuple-element.6.recv, bf16[256,256]{1,0:T(8,128)(2,1)S(1)} %copy-done.1, bf16[256,256]{1,0:T(8,128)(2,1)S(1)} %copy-done, f32[4,512,128]{2,1,0:T(8,128)S(1)} %get-tuple-element.7.nxt), custom_call_target="tpu_custom_call" | custom-call | tf_op jit(solution)/shard_map/field/pallas_call | solution.py:353
Async XLA Ops:
  1.3 35.4 %copy-start = (bf16[256,256]{1,0:T(8,128)(2,1)S(1)}, bf16[256,256]{1,0:T(8,128)(2,1)}, u32[]{:S(2)}) copy-start(bf16[256,256]{1,0:T(8,128)(2,1)} %constant.8.clone.tl) | copy-start | bytes 393220
  1.3 35.4 %copy-start.1 = (bf16[256,256]{1,0:T(8,128)(2,1)S(1)}, bf16[256,256]{1,0:T(8,128)(2,1)}, u32[]{:S(2)}) copy-start(bf16[256,256]{1,0:T(8,128)(2,1)} %constant.7.clone.th) | copy-start | bytes 393220

commit v4 on v3

--- a/solution.py
+++ b/solution.py
@@ -23,7 +23,8 @@
 ZB = 16
 GX, GY, GZ = 128, 128, 512
 ROWS = KY * ZB
-PAIRS = ((1, 7), (0, 2), (6, 3), (5, 4))
+PAIRS = ((1, 7), (2, 6), (4, 3), (5, 0))
+ORDER = ((1, (2, 1, 3)), (7, (2, 1, 3)), (2, (2, 1, 3, 0)), (6, (2, 1, 3, 0)), (4, (2, 1, 3, 0)), (3, (2, 1, 3, 0)), (5, (2, 1, 3, 0)), (0, (2, 1, 3)), (1, (0,)), (7, (0,)))
 
 
 def split(value):
@@ -72,16 +73,17 @@
     def _():
         pl.semaphore_signal(barrier, inc=1, device_id={"dom": dom + 1}, device_id_type=MESH)
 
-    load_modes = pltpu.make_async_copy(modes_hbm, modes, in_sem.at[0])
-    load_prev = pltpu.make_async_copy(prev_hbm, prev, in_sem.at[1])
+    halves = [pl.ds(0, GZ // 2), pl.ds(GZ // 2, GZ // 2)]
+    load_modes = [
+        pltpu.make_async_copy(modes_hbm.at[:, kz], modes.at[:, kz], in_sem.at[i]) for i, kz in enumerate(halves)
+    ]
+    load_prev = pltpu.make_async_copy(prev_hbm, prev, in_sem.at[2])
     load_tz = [
         pltpu.make_async_copy(tz_hbm.at[(my_y + dy) % NY], tz.at[slot], tz_sem.at[slot])
         for slot, dy in enumerate(sum(PAIRS, ()))
     ]
-    load_modes.start()
-    for load in load_tz:
+    for load in [load_modes[0], load_tz[0], load_tz[1], load_modes[1]] + load_tz[2:] + [load_prev]:
         load.start()
-    load_prev.start()
 
     count = jnp.full((8, GX), extent_ref[0, 0]).astype(F32)
     count_x = jnp.concatenate([count] * (GX // 8), axis=0)
@@ -111,57 +113,55 @@
     has_upper = jnp.where(dom < doms - 1, 1.0, 0.0)
     spread = spread * jnp.where(upper, has_upper, has_lower)
 
-    load_modes.wait()
-    for ky in range(KY):
-        h, l = split(modes[ky])
-        high[:, ky * GX : (ky + 1) * GX] = h
-        low[:, ky * GX : (ky + 1) * GX] = l
+    def along_z(slots, kz):
+        th = jnp.concatenate([tz[slot, 0, :, kz] for slot in slots], axis=0)
+        tl = jnp.concatenate([tz[slot, 1, :, kz] for slot in slots], axis=0)
+        return dot3((th, tl), (high[kz, :], low[kz, :]))
+
+    def finish(slots, value):
+        value = jnp.concatenate([value[:, ky * GX : (ky + 1) * GX] for ky in range(KY)], axis=0)
+        value = dot3(split(value), table_x)
+        for half in range(2):
+            for ky in range(KY):
+                for x in range(NX):
+                    begin = ky * 2 * NX * ZB + (half * NX + x) * ZB
+                    send[slots[half] * NX + x, pl.ds(ky, ZB, stride=KY), :] = value[begin : begin + ZB]
 
     def make_pair(chunk):
         slots = (2 * chunk, 2 * chunk + 1)
         for slot in slots:
             load_tz[slot].wait()
-        th = jnp.concatenate([tz[slot, 0] for slot in slots], axis=0)
-        tl = jnp.concatenate([tz[slot, 1] for slot in slots], axis=0)
-        along_z = dot3((th, tl), (high[...], low[...]))
-        along_z = jnp.concatenate([along_z[:, ky * GX : (ky + 1) * GX] for ky in range(KY)], axis=0)
-        along_x = dot3(split(along_z), table_x)
+        finish(slots, along_z(slots, slice(0, GZ)))
+
+    load_tz[0].wait()
+    load_tz[1].wait()
+    first = jnp.zeros((2 * NX * ZB, KY * GX), F32)
+    for i in range(2):
+        load_modes[i].wait()
+        kz = slice(i * GZ // 2, (i + 1) * GZ // 2)
         for ky in range(KY):
-            for half in range(2):
-                for x in range(NX):
-                    begin = ky * 2 * NX * ZB + (half * NX + x) * ZB
-                    send[slots[half] * NX + x, pl.ds(ky, ZB, stride=KY), :] = along_x[begin : begin + ZB]
-
+            h, l = split(modes[ky, kz, :])
+            high[kz, ky * GX : (ky + 1) * GX] = h
+            low[kz, ky * GX : (ky + 1) * GX] = l
+        first += along_z((0, 1), kz)
+    finish((0, 1), first)
     def transfer(slot, dy, dx):
         x, y = (my_x + dx) % NX, (my_y + dy) % NY
-        index = dx * NY + dy
         return pltpu.make_async_remote_copy(
             src_ref=send.at[slot * NX + x],
             dst_ref=recv.at[me],
-            send_sem=send_sem.at[index],
-            recv_sem=recv_sem.at[index],
+            send_sem=send_sem,
+            recv_sem=recv_sem,
             device_id={"pencil": x * NY + y},
             device_id_type=MESH,
         )
 
     flat = sum(PAIRS, ())
-    keep = pltpu.make_async_copy(send.at[flat.index(0) * NX + my_x], recv.at[me], send_sem.at[0])
-
-    def send_row(dy):
-        slot = flat.index(dy)
-
-        def go(dx, carry):
-            transfer(slot, dy, dx).start()
-            return carry
-
-        lax.fori_loop(1 if dy == 0 else 0, NX, go, 0)
-        if dy == 0:
-            keep.start()
+    keep = pltpu.make_async_copy(send.at[flat.index(0) * NX + my_x], recv.at[me], in_sem.at[3])
 
     def tell(semaphore, other):
         pl.semaphore_signal(semaphore, inc=1, device_id={"pencil": other}, device_id_type=MESH)
 
-    make_pair(0)
     pl.semaphore_wait(barrier, 5 + (dom + doms - 1) // doms)
     tell(row_up.at[0], y_down)
     tell(row_down.at[0], y_up)
@@ -170,21 +170,22 @@
     def _():
         pl.semaphore_signal(above_in, inc=1, device_id={"dom": dom - 1}, device_id_type=MESH)
 
-    for step in range(4):
-        pl.semaphore_wait(row_up.at[step], 1)
-        if step < 3:
-            tell(row_up.at[step + 1], y_down)
-        send_row(step + 1)
-        if step < 3:
-            pl.semaphore_wait(row_down.at[step], 1)
-            if step < 2:
-                tell(row_down.at[step + 1], y_up)
-            send_row(NY - step - 1)
-        if step == 0:
-            make_pair(1)
-            send_row(0)
-        if step < 2:
-            make_pair(step + 2)
+    known, made = 0, 1
+    for dy, offsets in ORDER:
+        while known < min(dy, NY - dy):
+            pl.semaphore_wait(row_up.at[known], 1)
+            if known < 3:
+                tell(row_up.at[known + 1], y_down)
+                pl.semaphore_wait(row_down.at[known], 1)
+            if known < 2:
+                tell(row_down.at[known + 1], y_up)
+            known += 1
+        while made <= flat.index(dy) // 2:
+            make_pair(made)
+            made += 1
+        for dx in offsets:
+            transfer(flat.index(dy), dy, dx).start()
+    keep.start()
 
     columns = split(jnp.concatenate([own, swapped], axis=0))
     nt = (((1,), (1,)), ((), ()))
@@ -262,14 +263,11 @@
             next_out[ky, begin : begin + part, :] = jnp.where(mode_x < count_p, value, 0.0)
 
     keep.wait()
-    for dy in flat:
-        slot = flat.index(dy)
-
-        def done(dx, carry):
-            transfer(slot, dy, dx).wait()
-            return carry
-
-        lax.fori_loop(1 if dy == 0 else 0, NX, done, 0)
+    blocks = pl.ds(0, NP - 1)
+    pltpu.make_async_remote_copy(
+        src_ref=send.at[blocks], dst_ref=recv.at[blocks], send_sem=send_sem, recv_sem=recv_sem,
+        device_id={"pencil": y_up}, device_id_type=MESH,
+    ).wait()
 
 
 def field_kernel(recv, th, tl, nxt, field_out, nxt_out, field, sem):
@@ -310,6 +308,10 @@
     for z in range(2):
         pair[z, :, :, z, :] = along_y.T.reshape(GY, NP, KY)
     return host_split(along_z), host_split(pair.reshape(2 * GY, NP * 2 * KY))
+
+
+def in_hbm(value):
+    return pltpu.with_memory_space_constraint(value, pltpu.HBM)
 
 
 def local(modes_now, modes_prev, extents):
@@ -336,10 +338,10 @@
             pltpu.VMEM((KY, 8, GZ), F32),
             pltpu.VMEM((KY, 8, GZ), F32),
             pltpu.VMEM((KY, 8, GZ), F32),
-            pltpu.SemaphoreType.DMA((2,)),
+            pltpu.SemaphoreType.DMA((4,)),
             pltpu.SemaphoreType.DMA((NY,)),
-            pltpu.SemaphoreType.DMA((NP,)),
-            pltpu.SemaphoreType.DMA((NP,)),
+            pltpu.SemaphoreType.DMA,
+            pltpu.SemaphoreType.DMA,
             pltpu.SemaphoreType.DMA((4,)),
             pltpu.SemaphoreType.REGULAR((4,)),
             pltpu.SemaphoreType.REGULAR((3,)),
@@ -349,7 +351,7 @@
             collective_id=0, has_side_effects=True, vmem_limit_bytes=24 * 1024 * 1024
         ),
         name="exchange",
-    )(*[pltpu.with_memory_space_constraint(v, pltpu.HBM) for v in (modes_now[0], modes_prev[0])], extents.reshape(1, 1), pltpu.with_memory_space_constraint(jnp.asarray(tz), pltpu.HBM))
+    )(in_hbm(modes_now[0]), in_hbm(modes_prev[0]), extents.reshape(1, 1), in_hbm(jnp.asarray(tz)))
     field, advanced = pl.pallas_call(
         field_kernel,
         out_shape=(

time: 38.3 us -> 36.1 us (0.943)
  the two profiles are of different devices: /device:TPU:200 before, /device:TPU:8 now
where the time goes in v4:
time: 36.1 us; the launch traced here: 36 us
  Pallas kernels  34.6 us (96%)
  between operations  1.32 us (4%)
    pallas_call x1, Pallas kernels, local(): pl.pallas_call(exchange_kernel, out_shape=(jax.ShapeDtypeStruct((NP, ROWS...  33.2 us
    pallas_call x1, Pallas kernels, local(): pl.pallas_call(field_kernel, out_shape=(jax.ShapeDtypeStruct((ZB, GY, GX)...  1.43 us

profile of v4, /device:TPU:8, one launch (start us, length us, event | category | flops | bytes accessed | tf_op | source)
XLA Modules:
  0.0 36.0 jit_solution(9510505081022903556)
XLA Ops:
  1.3 0.0 copy-start
  1.3 0.0 copy-start.1
  1.3 33.2 %exchange.1 = (f32[32,64,128]{2,1,0:T(8,128)S(1)}, f32[4,512,128]{2,1,0:T(8,128)S(1)}) custom-call(f32[4,512,128]{2,1,0:T(8,128)} %bitcast.6, f32[4,512,128]{2,1,0:T(8,128)} %bitcast.7, s32[1,1]{1,0:T(1,128)} %bitcast.5.extent_ref, bf16[8,2,64,512]{3,2,1,0:T(8,128)(2,1)} %constant.6.clone.tz_hbm), custom_call_target="tpu_custom_call" | custom-call | tf_op jit(solution)/shard_map/exchange/pallas_call | solution.py:322
  34.5 0.0 copy-done
  34.5 0.0 copy-done.1
  34.5 1.4 %field.1 = (f32[16,128,128]{2,1,0:T(8,128)}, f32[4,512,128]{2,1,0:T(8,128)}) custom-call(f32[32,64,128]{2,1,0:T(8,128)S(1)} %get-tuple-element.6.recv, bf16[256,256]{1,0:T(8,128)(2,1)S(1)} %copy-done.1, bf16[256,256]{1,0:T(8,128)(2,1)S(1)} %copy-done, f32[4,512,128]{2,1,0:T(8,128)S(1)} %get-tuple-element.7.nxt), custom_call_target="tpu_custom_call" | custom-call | tf_op jit(solution)/shard_map/field/pallas_call | solution.py:355
Async XLA Ops:
  1.3 33.2 %copy-start = (bf16[256,256]{1,0:T(8,128)(2,1)S(1)}, bf16[256,256]{1,0:T(8,128)(2,1)}, u32[]{:S(2)}) copy-start(bf16[256,256]{1,0:T(8,128)(2,1)} %constant.8.clone.tl) | copy-start | bytes 393220
  1.3 33.2 %copy-start.1 = (bf16[256,256]{1,0:T(8,128)(2,1)S(1)}, bf16[256,256]{1,0:T(8,128)(2,1)}, u32[]{:S(2)}) copy-start(bf16[256,256]{1,0:T(8,128)(2,1)} %constant.7.clone.th) | copy-start | bytes 393220

commit v5 on v4

--- a/solution.py
+++ b/solution.py
@@ -23,8 +23,8 @@
 ZB = 16
 GX, GY, GZ = 128, 128, 512
 ROWS = KY * ZB
-PAIRS = ((1, 7), (2, 6), (4, 3), (5, 0))
-ORDER = ((1, (2, 1, 3)), (7, (2, 1, 3)), (2, (2, 1, 3, 0)), (6, (2, 1, 3, 0)), (4, (2, 1, 3, 0)), (3, (2, 1, 3, 0)), (5, (2, 1, 3, 0)), (0, (2, 1, 3)), (1, (0,)), (7, (0,)))
+PAIRS = ((1, 7), (2, 6), (3, 5), (4, 0))
+ORDER = ((1, (2, 1, 3)), (7, (2, 1, 3)), (2, (2, 1, 3, 0)), (6, (2, 1, 3, 0)), (3, (2, 1)), (5, (2, 1)), (4, (2, 1, 3, 0)), (3, (3, 0)), (5, (3, 0)), (0, (2, 1, 3)), (1, (0,)), (7, (0,)))
 
 
 def split(value):
@@ -65,8 +65,8 @@
     y_up, y_down = my_x * NY + (my_y + 1) % NY, my_x * NY + (my_y + NY - 1) % NY
 
     barrier = pltpu.get_barrier_semaphore()
-    row_peers = [((my_x + dx) % NX) * NY + my_y for dx in (2, 1, 3)]
-    for other in row_peers + [y_up, y_down]:
+    for dx, dy in [(0, 1), (0, 7), (2, 0), (1, 0), (3, 0), (2, 1), (2, 7), (1, 1), (1, 7), (3, 1), (3, 7)]:
+        other = ((my_x + dx) % NX) * NY + (my_y + dy) % NY
         pl.semaphore_signal(barrier, inc=1, device_id={"pencil": other}, device_id_type=MESH)
 
     @pl.when(dom < doms - 1)
@@ -162,7 +162,7 @@
     def tell(semaphore, other):
         pl.semaphore_signal(semaphore, inc=1, device_id={"pencil": other}, device_id_type=MESH)
 
-    pl.semaphore_wait(barrier, 5 + (dom + doms - 1) // doms)
+    pl.semaphore_wait(barrier, 11 + (dom + doms - 1) // doms)
     tell(row_up.at[0], y_down)
     tell(row_down.at[0], y_up)
 
@@ -170,19 +170,19 @@
     def _():
         pl.semaphore_signal(above_in, inc=1, device_id={"dom": dom - 1}, device_id_type=MESH)
 
-    known, made = 0, 1
+    known, made = 1, 1
     for dy, offsets in ORDER:
-        while known < min(dy, NY - dy):
-            pl.semaphore_wait(row_up.at[known], 1)
-            if known < 3:
-                tell(row_up.at[known + 1], y_down)
-                pl.semaphore_wait(row_down.at[known], 1)
-            if known < 2:
-                tell(row_down.at[known + 1], y_up)
-            known += 1
         while made <= flat.index(dy) // 2:
             make_pair(made)
             made += 1
+        while known < min(dy, NY - dy):
+            pl.semaphore_wait(row_up.at[known - 1], 1)
+            if known < 3:
+                tell(row_up.at[known], y_down)
+                pl.semaphore_wait(row_down.at[known - 1], 1)
+            if known < 2:
+                tell(row_down.at[known], y_up)
+            known += 1
         for dx in offsets:
             transfer(flat.index(dy), dy, dx).start()
     keep.start()
@@ -343,8 +343,8 @@
             pltpu.SemaphoreType.DMA,
             pltpu.SemaphoreType.DMA,
             pltpu.SemaphoreType.DMA((4,)),
-            pltpu.SemaphoreType.REGULAR((4,)),
             pltpu.SemaphoreType.REGULAR((3,)),
+            pltpu.SemaphoreType.REGULAR((2,)),
             pltpu.SemaphoreType.REGULAR,
         ],
         compiler_params=pltpu.CompilerParams(

time: 36.1 us -> 34.6 us (0.958)
  the two profiles are of different devices: /device:TPU:8 before, /device:TPU:200 now
where the time goes in v5:
time: 34.6 us; the launch traced here: 34.4 us
  Pallas kernels  33.1 us (96%)
  between operations  1.32 us (4%)
    pallas_call x1, Pallas kernels, local(): pl.pallas_call(exchange_kernel, out_shape=(jax.ShapeDtypeStruct((NP, ROWS...  31.7 us
    pallas_call x1, Pallas kernels, local(): pl.pallas_call(field_kernel, out_shape=(jax.ShapeDtypeStruct((ZB, GY, GX)...  1.43 us

profile of v5, /device:TPU:200, one launch (start us, length us, event | category | flops | bytes accessed | tf_op | source)
XLA Modules:
  0.0 34.4 jit_solution(3711474128146660908)
XLA Ops:
  1.3 0.0 copy-start
  1.3 0.0 copy-start.1
  1.3 31.7 %exchange.1 = (f32[32,64,128]{2,1,0:T(8,128)S(1)}, f32[4,512,128]{2,1,0:T(8,128)S(1)}) custom-call(f32[4,512,128]{2,1,0:T(8,128)} %bitcast.6, f32[4,512,128]{2,1,0:T(8,128)} %bitcast.7, s32[1,1]{1,0:T(1,128)} %bitcast.5.extent_ref, bf16[8,2,64,512]{3,2,1,0:T(8,128)(2,1)} %constant.6.clone.tz_hbm), custom_call_target="tpu_custom_call" | custom-call | tf_op jit(solution)/shard_map/exchange/pallas_call | solution.py:322
  33.0 0.0 copy-done
  33.0 0.0 copy-done.1
  33.0 1.4 %field.1 = (f32[16,128,128]{2,1,0:T(8,128)}, f32[4,512,128]{2,1,0:T(8,128)}) custom-call(f32[32,64,128]{2,1,0:T(8,128)S(1)} %get-tuple-element.6.recv, bf16[256,256]{1,0:T(8,128)(2,1)S(1)} %copy-done.1, bf16[256,256]{1,0:T(8,128)(2,1)S(1)} %copy-done, f32[4,512,128]{2,1,0:T(8,128)S(1)} %get-tuple-element.7.nxt), custom_call_target="tpu_custom_call" | custom-call | tf_op jit(solution)/shard_map/field/pallas_call | solution.py:355
Async XLA Ops:
  1.3 31.7 %copy-start = (bf16[256,256]{1,0:T(8,128)(2,1)S(1)}, bf16[256,256]{1,0:T(8,128)(2,1)}, u32[]{:S(2)}) copy-start(bf16[256,256]{1,0:T(8,128)(2,1)} %constant.8.clone.tl) | copy-start | bytes 393220
  1.3 31.7 %copy-start.1 = (bf16[256,256]{1,0:T(8,128)(2,1)S(1)}, bf16[256,256]{1,0:T(8,128)(2,1)}, u32[]{:S(2)}) copy-start(bf16[256,256]{1,0:T(8,128)(2,1)} %constant.7.clone.th) | copy-start | bytes 393220

commit v6 on v5

--- a/solution.py
+++ b/solution.py
@@ -24,7 +24,7 @@
 GX, GY, GZ = 128, 128, 512
 ROWS = KY * ZB
 PAIRS = ((1, 7), (2, 6), (3, 5), (4, 0))
-ORDER = ((1, (2, 1, 3)), (7, (2, 1, 3)), (2, (2, 1, 3, 0)), (6, (2, 1, 3, 0)), (3, (2, 1)), (5, (2, 1)), (4, (2, 1, 3, 0)), (3, (3, 0)), (5, (3, 0)), (0, (2, 1, 3)), (1, (0,)), (7, (0,)))
+ORDER = ((1, (2, 1, 3)), (7, (2, 1, 3)), (2, (2, 1, 3)), (6, (2, 1, 3)), (3, (2, 1)), (5, (2, 1)), (4, (2, 1, 3, 0)), (3, (3, 0)), (5, (3, 0)), (2, (0,)), (6, (0,)), (0, (2, 1, 3)), (1, (0,)), (7, (0,)))
 
 
 def split(value):

time: 34.6 us -> 34.7 us (level)
  the two profiles are of different devices: /device:TPU:200 before, /device:TPU:320 now
where the time goes in v6:
time: 34.7 us; the launch traced here: 34.6 us
  Pallas kernels  33.3 us (96%)
  between operations  1.32 us (4%)
    pallas_call x1, Pallas kernels, local(): pl.pallas_call(exchange_kernel, out_shape=(jax.ShapeDtypeStruct((NP, ROWS...  31.9 us
    pallas_call x1, Pallas kernels, local(): pl.pallas_call(field_kernel, out_shape=(jax.ShapeDtypeStruct((ZB, GY, GX)...  1.43 us

profile of v6, /device:TPU:320, one launch (start us, length us, event | category | flops | bytes accessed | tf_op | source)
XLA Modules:
  0.0 34.6 jit_solution(14402475179453775439)
XLA Ops:
  1.3 0.0 copy-start
  1.3 0.0 copy-start.1
  1.3 31.9 %exchange.1 = (f32[32,64,128]{2,1,0:T(8,128)S(1)}, f32[4,512,128]{2,1,0:T(8,128)S(1)}) custom-call(f32[4,512,128]{2,1,0:T(8,128)} %bitcast.6, f32[4,512,128]{2,1,0:T(8,128)} %bitcast.7, s32[1,1]{1,0:T(1,128)} %bitcast.5.extent_ref, bf16[8,2,64,512]{3,2,1,0:T(8,128)(2,1)} %constant.6.clone.tz_hbm), custom_call_target="tpu_custom_call" | custom-call | tf_op jit(solution)/shard_map/exchange/pallas_call | solution.py:322
  33.2 0.0 copy-done
  33.2 0.0 copy-done.1
  33.2 1.4 %field.1 = (f32[16,128,128]{2,1,0:T(8,128)}, f32[4,512,128]{2,1,0:T(8,128)}) custom-call(f32[32,64,128]{2,1,0:T(8,128)S(1)} %get-tuple-element.6.recv, bf16[256,256]{1,0:T(8,128)(2,1)S(1)} %copy-done.1, bf16[256,256]{1,0:T(8,128)(2,1)S(1)} %copy-done, f32[4,512,128]{2,1,0:T(8,128)S(1)} %get-tuple-element.7.nxt), custom_call_target="tpu_custom_call" | custom-call | tf_op jit(solution)/shard_map/field/pallas_call | solution.py:355
Async XLA Ops:
  1.3 31.9 %copy-start = (bf16[256,256]{1,0:T(8,128)(2,1)S(1)}, bf16[256,256]{1,0:T(8,128)(2,1)}, u32[]{:S(2)}) copy-start(bf16[256,256]{1,0:T(8,128)(2,1)} %constant.8.clone.tl) | copy-start | bytes 393220
  1.3 31.9 %copy-start.1 = (bf16[256,256]{1,0:T(8,128)(2,1)S(1)}, bf16[256,256]{1,0:T(8,128)(2,1)}, u32[]{:S(2)}) copy-start(bf16[256,256]{1,0:T(8,128)(2,1)} %constant.7.clone.th) | copy-start | bytes 393220
